TPU v7x, 512 devices: a whole 4x4x16 slice. The times are simulated.
512 devices in a mesh: dp: 8 (over x, core), vocab: 64 (over z, y).
Axes of the slice: x: 4, y: 4, z: 16, core: 2. Of those that a mesh axis runs over, the one named last changes fastest.
Arguments:
- hidden_states: bfloat16 [1280, 4096], P('dp', 'vocab'), may hold values from -40 to 40
- head_weight: bfloat16 [10240, 4096], P('vocab'), may hold values from -1 to 1
- cluster_weight: bfloat16 [2, 4096], replicated, may hold values from -0.09375 to 0.09375
- proj_one: bfloat16 [4096, 1024], P('vocab'), may hold values from -1 to 1
- tail_one: bfloat16 [20480, 1024], P('vocab'), may hold values from -4 to 4
- proj_two: bfloat16 [4096, 256], P('vocab'), may hold values from -1 to 1
- tail_two: bfloat16 [106496, 256], P('vocab'), may hold values from -4 to 4
- targets: int32 [1280], P('dp'), may hold values from 0 to 106495, as said below
- token_cluster: int32 [1280], P('dp'), may hold values from 0 to 2, as said below
- tail_rows: int32 [8, 2, 40], P('dp'), may hold values from 0 to 159, as said below
- tail_counts: int32 [8, 2], P('dp'), may hold values from 20 to 40, as said below
Outputs:
- token_loss: float32 [1280], P('dp')
- grad_hidden: float32 [1280, 4096], P('dp', 'vocab')
- grad_head: float32 [10240, 4096], P('vocab', 'dp')
- grad_cluster: float32 [2, 4096], replicated
- grad_proj_one: float32 [4096, 1024], P('vocab')
- grad_tail_one: float32 [20480, 1024], P('vocab', 'dp')
- grad_proj_two: float32 [4096, 256], P('vocab')
- grad_tail_two: float32 [106496, 256], P('vocab', 'dp')
Inputs may be any that keep to these rules, and one draw needn't show every extreme that they name: `tail_counts`: for each tail cluster some group has all 40 slots live. `tail_rows`: live slots of group g and tail cluster c name distinct tokens of group g whose token_cluster is c + 1; dead slots hold 0. `token_cluster`: group g has exactly tail_counts[g, c] tokens of cluster c + 1, those named in tail_rows. `targets`: below 10240 for cluster 0, below 20480 for cluster 1, below 106496 for cluster 2.
All inputs are finite; a program needn't handle non-finite values.
Results may differ from a plain program's by a relative error of at most 0.0038.
Values may be sent and summed in bfloat16 or wider, within the bound.
A program may use at most 64 MiB of HBM per device.

v0:
```python
import jax
import jax.numpy as jnp
from jax import lax
from jax.sharding import PartitionSpec as P

loss_scale = 64.0
contract_last = (((1,), (1,)), ((), ()))
contract_first = (((0,), (0,)), ((), ()))


def joined(value, axis, join):
    pieces = jax.tree.map(lambda part: lax.all_gather(part, axis), value)
    head = jax.tree.map(lambda part: part[0], pieces)
    tail = jax.tree.map(lambda part: part[1:], pieces)
    total, _ = lax.scan(lambda total, slab: (join(total, slab), None), head, tail)
    return total


def slice_stats(logits, is_target):
    highest = jnp.max(logits, axis=1)
    summed = jnp.sum(jnp.exp(logits - highest[:, None]), axis=1)
    chosen = jnp.sum(jnp.where(is_target, logits, 0.0), axis=1)
    return (highest, summed, chosen)


def join_stats(first, second):
    highest = jnp.maximum(first[0], second[0])
    summed = first[1] * jnp.exp(first[0] - highest) + second[1] * jnp.exp(second[0] - highest)
    return (highest, summed, first[2] + second[2])


def join_all(first, second):
    merged = ()
    for position in range(0, len(first), 3):
        merged = merged + join_stats(
            first[position : position + 3], second[position : position + 3]
        )
    return merged


def on_device(
    hidden_states,
    head_weight,
    cluster_weight,
    proj_one,
    tail_one,
    proj_two,
    tail_two,
    targets,
    token_cluster,
    tail_rows,
    tail_counts,
):
    vocab_count = lax.axis_size("vocab")
    vocab_index = lax.axis_index("vocab")
    group_count = lax.axis_size("dp")
    group_index = lax.axis_index("dp")
    slice_width = hidden_states.shape[1]
    head_rows = head_weight.shape[0]
    head_size = head_rows * vocab_count
    slot_count = tail_rows.shape[2]
    whole = lax.all_gather(hidden_states, "vocab", axis=1, tiled=True)
    head_logits = lax.dot_general(
        whole, head_weight, contract_last, preferred_element_type=jnp.float32
    )
    entry_logits = lax.dot_general(
        whole, cluster_weight, contract_last, preferred_element_type=jnp.float32
    )
    head_target = jnp.where(token_cluster == 0, targets, head_size + token_cluster - 1)
    head_hit = (
        lax.broadcasted_iota(jnp.int32, head_logits.shape, 1)
        == (head_target - vocab_index * head_rows)[:, None]
    )
    head_stats = slice_stats(head_logits, head_hit)
    head_stats = joined(head_stats, "vocab", join_all)
    tails = ((proj_one, tail_one), (proj_two, tail_two))
    slot_ids = jnp.arange(slot_count, dtype=jnp.int32)
    row_lists = []
    usable_list = []
    gathered_rows = []
    partial_sums = []
    for cluster in range(2):
        row_ids = tail_rows[0, cluster]
        row_lists.append(row_ids)
        usable_list.append(slot_ids < tail_counts[0, cluster])
        chosen_rows = hidden_states[row_ids]
        gathered_rows.append(chosen_rows)
        partial_sums.append(
            jnp.dot(chosen_rows, tails[cluster][0], preferred_element_type=jnp.float32)
        )
    projected_sums = lax.psum((partial_sums[0], partial_sums[1]), "vocab")
    tail_stats = ()
    tail_logits = []
    tail_hits = []
    projected_list = []
    for cluster in range(2):
        projected_rows = projected_sums[cluster].astype(jnp.bfloat16)
        projected_list.append(projected_rows)
        embedding = tails[cluster][1]
        logits = lax.dot_general(
            projected_rows, embedding, contract_last, preferred_element_type=jnp.float32
        )
        goal_ids = (
            jnp.where(usable_list[cluster], targets[row_lists[cluster]], 0)
            - vocab_index * embedding.shape[0]
        )
        is_target = lax.broadcasted_iota(jnp.int32, logits.shape, 1) == goal_ids[:, None]
        tail_logits.append(logits)
        tail_hits.append(is_target)
        tail_stats = tail_stats + slice_stats(logits, is_target)
    tail_stats = joined(tail_stats, "vocab", join_all)
    highest = jnp.maximum(head_stats[0], jnp.max(entry_logits, axis=1))
    summed = head_stats[1] * jnp.exp(head_stats[0] - highest) + jnp.sum(
        jnp.exp(entry_logits - highest[:, None]), axis=1
    )
    head_total = highest + jnp.log(summed)
    entry_hit = token_cluster[:, None] == jnp.arange(1, 3, dtype=jnp.int32)[None, :]
    chosen = head_stats[2] + jnp.sum(jnp.where(entry_hit, entry_logits, 0.0), axis=1)
    token_loss = head_total - chosen
    head_grad = (
        loss_scale * (jnp.exp(head_logits - head_total[:, None]) - head_hit.astype(jnp.float32))
    ).astype(jnp.bfloat16)
    entry_grad = (
        loss_scale * (jnp.exp(entry_logits - head_total[:, None]) - entry_hit.astype(jnp.float32))
    ).astype(jnp.bfloat16)
    head_product = lax.dot_general(
        head_grad, whole, contract_first, preferred_element_type=jnp.float32
    )
    head_part = lax.optimization_barrier(head_product.astype(jnp.bfloat16)).astype(jnp.float32)
    entry_part = lax.dot_general(
        entry_grad, whole, contract_first, preferred_element_type=jnp.float32
    )
    entry_slice = lax.dynamic_slice_in_dim(
        cluster_weight, vocab_index * slice_width, slice_width, 1
    )
    grad_hidden = jnp.dot(entry_grad, entry_slice, preferred_element_type=jnp.float32)
    columns = lax.all_to_all(head_weight, "vocab", split_axis=1, concat_axis=0, tiled=True)
    grad_hidden = grad_hidden + jnp.dot(
        lax.all_gather(head_grad, "vocab", axis=1, tiled=True),
        columns,
        preferred_element_type=jnp.float32,
    )
    grad_list = []
    back_parts = []
    for cluster in range(2):
        cluster_stats = tail_stats[3 * cluster : 3 * cluster + 3]
        tail_total = cluster_stats[0] + jnp.log(cluster_stats[1])
        usable = usable_list[cluster]
        token_loss = token_loss.at[row_lists[cluster]].add(
            jnp.where(usable, tail_total - cluster_stats[2], 0.0)
        )
        tail_grad = jnp.where(
            usable[:, None],
            loss_scale
            * (
                jnp.exp(tail_logits[cluster] - tail_total[:, None])
                - tail_hits[cluster].astype(jnp.float32)
            ),
            0.0,
        ).astype(jnp.bfloat16)
        grad_list.append(tail_grad)
        back_parts.append(jnp.dot(tail_grad, tails[cluster][1], preferred_element_type=jnp.float32))
    back_sums = lax.psum((back_parts[0], back_parts[1]), "vocab")
    proj_parts = []
    for cluster in range(2):
        back_rows = back_sums[cluster].astype(jnp.bfloat16)
        proj_parts.append(
            lax.dot_general(
                gathered_rows[cluster],
                back_rows,
                contract_first,
                preferred_element_type=jnp.float32,
            )
        )
        grad_hidden = grad_hidden.at[row_lists[cluster]].add(
            lax.dot_general(
                back_rows, tails[cluster][0], contract_last, preferred_element_type=jnp.float32
            )
        )
    table_start = (
        jnp.zeros((tail_one.shape[0], tail_one.shape[1] // group_count), jnp.float32),
        jnp.zeros((tail_two.shape[0], tail_two.shape[1] // group_count), jnp.float32),
    )
    pieces = (
        lax.all_gather(grad_list[0], "dp", axis=0, tiled=True),
        lax.all_gather(grad_list[1], "dp", axis=0, tiled=True),
        lax.all_gather(projected_list[0], "dp", axis=0, tiled=True),
        lax.all_gather(projected_list[1], "dp", axis=0, tiled=True),
    )
    results = []
    for grads, projected_piece, total in (
        (pieces[0], pieces[2], table_start[0]),
        (pieces[1], pieces[3], table_start[1]),
    ):
        width = total.shape[1]
        columns_here = lax.dynamic_slice_in_dim(projected_piece, group_index * width, width, 1)
        blocks = grads.shape[0] // slot_count
        product = jnp.einsum(
            "gct,gcd->gtd",
            grads.reshape(blocks, slot_count, grads.shape[1]),
            columns_here.reshape(blocks, slot_count, width),
            preferred_element_type=jnp.float32,
        )
        rounded = lax.optimization_barrier(product.astype(jnp.bfloat16)).astype(jnp.float32)
        results.append(jnp.sum(rounded, axis=0))
    head_grads = lax.psum_scatter(head_part, "dp", scatter_dimension=1, tiled=True)
    small_grads = lax.psum((proj_parts[0], proj_parts[1], entry_part), "dp")
    return (
        token_loss,
        grad_hidden,
        head_grads,
        small_grads[2],
        small_grads[0],
        results[0],
        small_grads[1],
        results[1],
    )


def solution(mesh):
    return jax.shard_map(
        on_device,
        mesh=mesh,
        in_specs=(
            P("dp", "vocab"),
            P("vocab", None),
            P(),
            P("vocab", None),
            P("vocab", None),
            P("vocab", None),
            P("vocab", None),
            P("dp"),
            P("dp"),
            P("dp", None, None),
            P("dp", None),
        ),
        out_specs=(
            P("dp"),
            P("dp", "vocab"),
            P("vocab", "dp"),
            P(),
            P("vocab", None),
            P("vocab", "dp"),
            P("vocab", None),
            P("vocab", "dp"),
        ),
        check_vma=False,
    )
```

profile of v0, /device:TPU:1, one launch (start us, length us, event | category | flops | bytes accessed | tf_op | source)
XLA Modules:
  0.0 1280.2 jit_solution(75088916503100888)
XLA Ops:
  8.0 0.9 copy.30
  10.8 1.5 gather_fusion.3
  12.3 1.5 gather_fusion.1
  13.8 1.1 fusion.39
  14.8 0.9 fusion.40
  15.7 1.3 fusion.34
  17.1 1.3 dynamic-slice
  18.3 231.8 %all-reduce.18 = (bf16[40,1024]{1,0:T(8,128)(2,1)S(1)}, bf16[40,256]{1,0:T(8,128)(2,1)S(1)}) all-reduce(f32[40,1024]{1,0:T(8,128)S(1)} %fusion.39, f32[40,256]{1,0:T(8,128)S(1)} %fusion.40), channel_id=1, replica_groups=mesh['dp'=8,'vocab'=64] {'vocab'}, use_global_device_ids=true, to_apply=%region_8.9 | all-reduce | flops 51200 | bytes 307200 | tf_op jit(solution)/shard_map/psum | solution.py:91
  250.2 1.5 fusion.36
  252.7 1.3 select_subtract_fusion
  256.4 219.8 %all-reduce.10 = (f32[2560]{0:T(1024)S(1)}, f32[2560]{0:T(1024)S(1)}, f32[2560]{0:T(1024)S(1)}, f32[2560]{0:T(1024)S(1)}, f32[2560]{0:T(1024)S(1)}, /*index=5*/f32[2560]{0:T(1024)S(1)}) all-reduce(f32[2560]{0:T(1024)S(1)} %dynamic-update-slice.3, f32[2560]{0:T(1024)S(1)} %dynamic-update-slice.4, ...), channel_id=5, replica_groups=mesh['dp'=8,'vocab'=64] {'vocab'}, use_global_device_ids=true, to_apply=%add.3 | all-reduce | flops 15360 | bytes 122880
  477.1 4.6 while.35
  482.3 1.2 subtract_select_fusion
  485.1 1.2 fusion.42
  487.5 1.2 subtract_select_fusion.1
  489.1 2.7 fusion.35
  493.5 1.4 dynamic-update-slice.2
  494.9 222.6 %all-reduce.19 = (f32[10240]{0:T(1024)}, f32[10240]{0:T(1024)}, f32[10240]{0:T(1024)}, bf16[40,1024]{1,0:T(8,128)(2,1)S(1)}, bf16[40,256]{1,0:T(8,128)(2,1)}) all-reduce(f32[10240]{0:T(1024)} %copy-done.8, f32[10240]{0:T(1024)} %copy-done.7, f32[10240]{0:T(1024)} %dynamic-update-slice.2, ...), channel_id=2, replica_groups=mesh['dp'=8,'vocab'=64] {'vocab'}, use_global_device_ids=true, to_apply=%add | all-reduce | flops 81920 | bytes 552960
  718.3 0.9 slice.117
  719.8 0.9 slice.118
  721.4 0.9 slice.119
  723.7 91.3 %while.34 = (s32[]{:T(128)}, f32[160]{0:T(256)S(1)}, f32[160]{0:T(256)S(1)}, f32[160]{0:T(256)S(1)}, f32[63,160]{1,0:T(8,128)}, /*index=5*/f32[63,160]{1,0:T(8,128)}, f32[63,160]{1,0:T(8,128)S(1)}, s32[]{:T(128)}) while((s32[]{:T(128)}, f32[160]{0:T(256)S(1)}, f32[160]{0:T(256)S(1)}, f32[160]{0:T(256)S(1)}, f32[63,160]{1,0:T(8,128)}, ...), condition=%wide.region_4.5_spmd, body=%wide.region_3.4_spmd.sunk | while | flops 1122 | bytes 9701 | solution.py:15
  815.1 1.1 fusion.38
  817.7 3.7 copy.38
  821.4 6.4 all-to-all-start
  827.8 0.8 fusion.46
  828.6 0.9 fusion.44
  829.6 0.9 convolution_convert_fusion
  830.5 1.8 convert_element_type.67
  832.3 194.3 %all_gather.92 = bf16[320,320]{1,0:T(8,128)(2,1)S(1)} all-gather(bf16[40,320]{1,0:T(8,128)(2,1)S(1)} %select_convert_fusion.1), channel_id=1, replica_groups=mesh['dp'=8,'vocab'=64] {'dp'}, dimensions={0}, use_global_device_ids=true | all-gather | bytes 230400 | tf_op jit(solution)/shard_map/all_gather | solution.py:185
  1026.6 13.2 %all_gather.93 = bf16[320,1024]{1,0:T(8,128)(2,1)S(1)} all-gather(bf16[40,1024]{1,0:T(8,128)(2,1)S(1)} %get-tuple-element.203), channel_id=1, replica_groups=mesh['dp'=8,'vocab'=64] {'dp'}, dimensions={0}, use_global_device_ids=true | all-gather | bytes 737280 | tf_op jit(solution)/shard_map/all_gather | solution.py:187
  1039.9 1.3 convolution_convert_fusion.2
  1041.1 13.1 %all_gather.95 = bf16[320,256]{1,0:T(8,128)(2,1)S(1)} all-gather(bf16[40,256]{1,0:T(8,128)(2,1)S(1)} %copy-done.12), channel_id=1, replica_groups=mesh['dp'=8,'vocab'=64] {'dp'}, dimensions={0}, use_global_device_ids=true | all-gather | bytes 184320 | tf_op jit(solution)/shard_map/all_gather | solution.py:188
  1054.3 1.9 convert_reduce_fusion.1
  1056.1 1.7 convolution_convert_fusion.1
  1058.6 0.8 scatter_fusion
  1059.4 0.8 scatter_fusion.1
  1060.9 23.4 %psum.53 = f32[2,4096]{1,0:T(2,128)} all-reduce(f32[2,4096]{1,0:T(2,128)S(1)} %fusion.29), channel_id=1, replica_groups=mesh['dp'=8,'vocab'=64] {'dp'}, use_global_device_ids=true, to_apply=%region_25.26 | all-reduce | flops 8192 | bytes 65536 | tf_op jit(solution)/shard_map/psum | solution.py:207
  1084.6 2.8 copy.33
  1087.4 4.3 all_to_all.17
  1091.7 54.1 %all-gather.15.cloned.1.call-done = bf16[160,10240]{0,1:T(8,128)(2,1)} async-done(((bf16[160,160]{0,1:T(8,128)(2,1)}), bf16[160,10240]{0,1:T(8,128)(2,1)}) %all-gather.15.cloned.1.call-update) | async-done | bytes 3276816 | tf_op jit(solution)/shard_map/all_gather | solution.py:139
  1145.9 3.9 fusion.43
  1149.7 0.9 convolution_add_fusion
  1151.6 0.8 scatter_fusion.3
  1153.1 72.8 %all-reduce.17.cloned.1.call-done = (f32[64,1024]{1,0:T(8,128)}, f32[64,256]{1,0:T(8,128)}) async-done(((f32[64,1024]{1,0:T(8,128)}, f32[64,256]{1,0:T(8,128)}), (f32[64,1024]{1,0:T(8,128)}, f32[64,256]{1,0:T(8,128)})) %all-reduce.17.cloned.1.call-update) | async-done | bytes 327696 | tf_op jit(solution)/shard_map/psum | solution.py:207
  1225.9 44.6 %reduce-scatter.2.cloned.1.call-done = f32[160,512]{1,0:T(8,128)} async-done(((f32[160,4096]{1,0:T(8,128)}), f32[160,512]{1,0:T(8,128)}) %reduce-scatter.2.cloned.1.call-update) | async-done | bytes 327696 | tf_op jit(solution)/shard_map/reduce_scatter | solution.py:206
  1270.5 1.7 copy.100
  1272.2 1.5 copy.101
  (499 shorter events, 114.0 us)
Async XLA Ops:
  7.2 247.6 %copy-start = (bf16[1664,256]{1,0:T(8,128)(2,1)S(1)}, bf16[1664,256]{1,0:T(8,128)(2,1)}, u32[]{:S(2)}) copy-start(bf16[1664,256]{1,0:T(8,128)(2,1)} %param.21) | copy-start | bytes 2555908
  7.2 481.9 %all-gather.13.cloned.1.call-start = ((), (), s32[]{:S(2)}) async-start(), calls=%async_computation.2 | async-start | bytes 2129920 | tf_op jit(solution)/shard_map/all_gather | solution.py:62
  7.9 1048.2 %all-gather.17.cloned.1.call-start = ((), (), s32[]{:S(2)}) async-start(), calls=%async_computation.5 | async-start | bytes 1198080 | tf_op jit(solution)/shard_map/all_gather | solution.py:186
  9.6 4.2 copy-start.14
  250.2 236.1 %copy-start.11 = (bf16[40,256]{1,0:T(8,128)(2,1)}, bf16[40,256]{1,0:T(8,128)(2,1)S(1)}, u32[]{:S(2)}) copy-start(bf16[40,256]{1,0:T(8,128)(2,1)S(1)} %get-tuple-element.204) | copy-start | bytes 61444
  251.7 237.1 %copy-start.4 = (bf16[320,1024]{1,0:T(8,128)(2,1)S(1)}, bf16[320,1024]{1,0:T(8,128)(2,1)}, u32[]{:S(2)}) copy-start(bf16[320,1024]{1,0:T(8,128)(2,1)} %param.19) | copy-start | bytes 1966084
  255.3 233.8 %copy-start.2 = (s32[160]{0:T(256)S(1)}, s32[160]{0:T(256)}, u32[]{:S(2)}) copy-start(s32[160]{0:T(256)} %param.22) | copy-start | bytes 1924
  255.3 233.8 %copy-start.13 = (s32[160]{0:T(256)S(1)}, s32[160]{0:T(256)}, u32[]{:S(2)}) copy-start(s32[160]{0:T(256)} %param.23) | copy-start | bytes 1924
  484.4 661.5 %all-gather.15.cloned.1.call-start = ((), (), s32[]{:S(2)}) async-start(), calls=%async_computation.3 | async-start | bytes 5324800 | tf_op jit(solution)/shard_map/all_gather | solution.py:139
  489.1 326.0 %copy-start.3 = (bf16[160,4096]{0,1:T(8,128)(2,1)S(1)}, bf16[160,4096]{0,1:T(8,128)(2,1)}, u32[]{:S(2)}) copy-start(bf16[160,4096]{0,1:T(8,128)(2,1)} %all-gather.13.cloned.1.call-done) | copy-start | bytes 3932164
  492.1 0.6 copy-start.8
  492.9 0.6 copy-start.7
  821.4 6.4 copy-start.10
  821.4 8.3 copy-start.5
  821.4 263.2 %all-to-all-start = ((bf16[160,64,64]{0,2,1:T(8,128)(2,1)}), bf16[160,64,64]{0,2,1:T(8,128)(2,1)}, u32[]{:S(2)}, u32[]{:S(2)}) async-start(bf16[160,64,64]{0,2,1:T(8,128)(2,1)} %bitcast.100), calls=%async_computation | async-start | bytes 4194304 | tf_op jit(solution)/shard_map/all_to_all | solution.py:137
  827.8 398.2 %all-reduce.17.cloned.1.call-start = ((), (), s32[]{:S(2)}) async-start(), calls=%async_computation.6 | async-start | bytes 655360 | tf_op jit(solution)/shard_map/psum | solution.py:207
  829.6 441.0 %reduce-scatter.2.cloned.1.call-start = ((), (), s32[]{:S(2)}) async-start(), calls=%async_computation.4 | async-start | bytes 2949120 | tf_op jit(solution)/shard_map/reduce_scatter | solution.py:206
  832.3 208.8 %copy-start.12 = (bf16[40,256]{1,0:T(8,128)(2,1)S(1)}, bf16[40,256]{1,0:T(8,128)(2,1)}, u32[]{:S(2)}) copy-start(bf16[40,256]{1,0:T(8,128)(2,1)} %copy-done.11) | copy-start | bytes 61444
  1041.1 17.5 %copy-start.15 = (s32[40]{0:T(128)S(1)}, s32[40]{0:T(128)}, u32[]{:S(2)}) copy-start(s32[40]{0:T(128)} %copy-done.14) | copy-start | bytes 484
  1041.1 17.5 %copy-start.18 = (f32[40]{0:T(128)S(1)}, f32[40]{0:T(128)}, u32[]{:S(2)}) copy-start(f32[40]{0:T(128)} %get-tuple-element.215) | copy-start | bytes 484
  1056.1 3.3 copy-start.17
  1056.1 4.1 copy-start.16
  1058.6 25.7 %copy-start.9 = (bf16[64,256]{1,0:T(8,128)(2,1)S(1)}, bf16[64,256]{1,0:T(8,128)(2,1)}, u32[]{:S(2)}) copy-start(bf16[64,256]{1,0:T(8,128)(2,1)} %param.20) | copy-start | bytes 98308
  1058.6 25.8 %copy-start.6 = (bf16[64,1024]{1,0:T(8,128)(2,1)S(1)}, bf16[64,1024]{1,0:T(8,128)(2,1)}, u32[]{:S(2)}) copy-start(bf16[64,1024]{1,0:T(8,128)(2,1)} %param.18) | copy-start | bytes 393220
  1060.3 27.1 %copy-start.1 = (f32[160]{0:T(256)}, f32[160]{0:T(256)S(1)}, u32[]{:S(2)}) copy-start(f32[160]{0:T(256)S(1)} %scatter_fusion.1) | copy-start | bytes 1924
Sparse Core Ops, SparseCore 0:
  11.0 138.0 all-gather.12
  484.5 133.6 all-gather.16
  817.8 328.0 all-gather.14
  1148.7 77.1 all-reduce.16
  1229.4 41.0 reduce-scatter.1
where the time goes:
time: 1290 us; the launch traced here: 1280 us
  blocking collectives  918 us (71%)
  waiting for transfers between devices  172 us (13%)
  local copies, waits for them, and re-layouts  123 us (10%)
  other arithmetic  22.5 us (2%)
  matrix products  20.3 us (2%)
  between operations  15.6 us (1%)
    unnamed x2, blocking collectives  442 us
    psum x1, blocking collectives, on_device(): projected_sums = lax.psum((partial_sums[0], partial_sums[1]), 'vocab')  232 us
    all_gather x1, blocking collectives, on_device(): lax.all_gather(grad_list[0], 'dp', axis=0, tiled=True)  194 us
    dynamic_slice x126, local copies, waits for them, and re-layouts, joined(): lax.scan(lambda total, slab: (join(total, slab), None), head, tail)  88.7 us
    psum x1, waiting for transfers between devices, on_device(): small_grads = lax.psum((proj_parts[0], proj_parts[1], entry_part), 'dp')  72.8 us
    all_gather x1, waiting for transfers between devices, on_device(): lax.all_gather(head_grad, 'vocab', axis=1, tiled=True)  54.1 us
    reduce_scatter x1, waiting for transfers between devices, on_device(): lax.psum_scatter(head_part, 'dp', scatter_dimension=1, tiled=True)  44.6 us
  transfers between devices with their start and end apart: 6, of which 3 were waited for; matrix products, arithmetic and copies ran while one was open for 12% of the time, Pallas kernels for 0%

commit v1 on v0

v1 whole, which is shorter than its diff:
```python
import jax
import jax.numpy as jnp
from jax import lax
from jax.experimental import pallas as pl
from jax.experimental.pallas import tpu as pltpu
from jax.sharding import PartitionSpec as P

MESH = pl.DeviceIdType.MESH
F32 = jnp.float32
BF16 = jnp.bfloat16
SCALE = 64.0
FAR = (1, 2, 3)
NEAR = (1, 15, 2)
NEAR_FROM = (15, 1, 14)
SEMS = 128
NT = (((1,), (1,)), ((), ()))
TN = (((0,), (0,)), ((), ()))
NN = (((1,), (0,)), ((), ()))


def dot(a, b, dims=NN):
    return lax.dot_general(a, b, dims, preferred_element_type=F32)


def dot_exact(a, b):
    return lax.dot_general(a, b, NN, precision=lax.Precision.HIGHEST, preferred_element_type=F32)


def lanes(shape):
    return lax.broadcasted_iota(jnp.int32, shape, len(shape) - 1)


def rows_of(shape):
    return lax.broadcasted_iota(jnp.int32, shape, len(shape) - 2)


def pack_rest(rest, height):
    out = None
    total = rest.shape[0]
    for q in range(4):
        lo, hi = q * height, min((q + 1) * height, total)
        part = rest[lo:hi]
        if q:
            part = pltpu.roll(part, 32 * q, 1)
        if hi - lo < height:
            part = jnp.concatenate([part, jnp.zeros((height - (hi - lo), 128), F32)], axis=0)
        out = part if out is None else out + part
    return out


def unpack_rest(packed, q):
    part = packed if q == 0 else pltpu.roll(packed, 128 - 32 * q, 1)
    return jnp.where(lanes(part.shape) < 32, part, 0.0).astype(BF16)


def kernel(
    hid_ref, hw_ref, cw_ref, p1_ref, t1_ref, p2_ref, t2_ref, meta_ref,
    loss_ref, gh_ref, head_ref, cl_ref, gp1_ref, gt1_ref, gp2_ref, gt2_ref,
    hp, G, WT, hwx, hwxT, HG, HU,
    CH, PT, PRY, PRN, PRF, PS1, PS2, PG, Xf, PJ,
    P1f, P2f, P1b, P2b,
    ST, STF, STN, STY, TS,
    LG, L1s, L2s, INF, GP, GU, GC,
    BT, BRY, BRN, BRF, BS1, BS2, BG, BK, C1f, C2f,
    GB, GRY, GS1, GRN, GS2, GRF,
    ssem, rsem, lsem,
):
    d = lax.axis_index("dp")
    v = lax.axis_index("vocab")
    x, c = lax.div(d, 2), lax.rem(d, 2)
    z, y = lax.div(v, 4), lax.rem(v, 4)
    zhi, zlo = lax.div(z, 4), lax.rem(z, 4)

    def far_dev(k):
        return (d, lax.rem(z + 4 * k, 16) * 4 + y)

    def near_dev(o):
        return (d, lax.rem(z + o, 16) * 4 + y)

    def y_dev(k):
        return (d, z * 4 + lax.rem(y + k, 4))

    def x_dev(k):
        return (lax.rem(x + k, 4) * 2 + c, v)

    core_dev = (x * 2 + 1 - c, v)

    def dp_dev(k):
        return (lax.rem(d + k, 8), v)

    counter = [0]
    sent = []

    def send(src, dst, dev):
        i = counter[0]
        counter[0] += 1
        copy = pltpu.make_async_remote_copy(
            src_ref=src, dst_ref=dst, send_sem=ssem.at[i], recv_sem=rsem.at[i],
            device_id=dev, device_id_type=MESH,
        )
        copy.start()
        sent.append(copy)
        return i

    def recv(i, slot):
        pltpu.make_async_remote_copy(
            src_ref=slot, dst_ref=slot, send_sem=ssem.at[i], recv_sem=rsem.at[i],
            device_id=core_dev, device_id_type=MESH,
        ).wait_recv()

    hw_copy = pltpu.make_async_copy(hw_ref, hwx.at[0:160], lsem)
    hw_copy.start()

    barrier = pltpu.get_barrier_semaphore()
    greeted = 0
    for k in FAR:
        pl.semaphore_signal(barrier, inc=1, device_id=far_dev(k), device_id_type=MESH)
        pl.semaphore_signal(barrier, inc=1, device_id=y_dev(k), device_id_type=MESH)
        greeted += 2
    for o in NEAR_FROM:
        pl.semaphore_signal(barrier, inc=1, device_id=near_dev(o), device_id_type=MESH)
        greeted += 1
    for k in range(1, 8):
        pl.semaphore_signal(barrier, inc=1, device_id=dp_dev(k), device_id_type=MESH)
        greeted += 1

    hp[...] = jnp.zeros_like(hp)
    hp[:, 0:160] = hid_ref[...].astype(F32)
    G[y, zlo, zhi, 0:64, :] = hp[:, 0:128].astype(BF16)
    G[y, zlo, zhi, 64:80, :] = pack_rest(hp[:, 128:256], 16).astype(BF16)

    TS[...] = jnp.zeros_like(TS)
    TS[0:8, :] = meta_ref[:, 256:384].astype(F32)
    row_col = jnp.transpose(TS[...])[0:80, 0:1].astype(jnp.int32)
    target = meta_ref[0:1, 0:256]
    cluster = meta_ref[1:2, 0:256]
    slot_hit = lanes((80, 256)) == row_col
    onehot = jnp.where(slot_hit, 1.0, 0.0).astype(BF16)
    live = row_col >= 0
    goal = jnp.sum(jnp.where(slot_hit, target, 0).astype(F32), axis=1, keepdims=True).astype(jnp.int32)
    goal = jnp.where(live, goal, -1)

    hidb = hp[...].astype(BF16)
    chosen = dot(onehot, hidb, NT)
    CH[d, :, 64:128] = jnp.zeros((80, 64), BF16)
    CH[d, :, 0:64] = chosen.astype(BF16)
    part1 = dot(chosen[0:40].astype(BF16), p1_ref[...])
    part2 = dot(chosen[40:80].astype(BF16), p2_ref[...])

    def to_tiles(tiles, a, b):
        for t in range(64):
            at = tiles.at[t // 16, (t // 4) % 4, t % 4]
            i, j = t // 10, t % 10
            if t >= 50:
                at[...] = jnp.zeros((8, 128), F32)
            elif j < 8:
                at[...] = a[8 * i : 8 * i + 8, 128 * j : 128 * j + 128]
            else:
                at[...] = b[8 * i : 8 * i + 8, 128 * j - 1024 : 128 * j - 896]

    to_tiles(PT, part1, part2)

    pl.semaphore_wait(barrier, greeted)

    own = G.at[y, zlo, zhi]
    hid_far = [send(own, own, far_dev(k)) for k in FAR]

    def small_y(tiles, slots):
        return [send(tiles.at[lax.rem(y + k, 4)], slots.at[k - 1], y_dev(k)) for k in FAR]

    def small_near(tiles, slots, ids, sums, nslots):
        for n, i in enumerate(ids):
            recv(i, slots.at[n])
        sums[...] = (tiles[y] + slots[0]) + (slots[1] + slots[2])
        return [
            send(sums.at[lax.rem(zlo + o, 4)], nslots.at[n], near_dev(o))
            for n, o in enumerate(NEAR)
        ]

    def small_far(sums, nslots, ids, sums2, fslots):
        for n, i in enumerate(ids):
            recv(i, nslots.at[n])
        sums2[...] = (sums[zlo] + nslots[0]) + (nslots[1] + nslots[2])
        return [
            send(sums2.at[lax.rem(zhi + k, 4)], fslots.at[k - 1], far_dev(k)) for k in FAR
        ]

    def small_back_far(sums2, fslots, ids, full):
        for n, i in enumerate(ids):
            recv(i, fslots.at[n])
        full[y, zlo, zhi] = (sums2[zhi] + fslots[0]) + (fslots[1] + fslots[2])
        return [send(full.at[y, zlo, zhi], full.at[y, zlo, zhi], far_dev(k)) for k in FAR]

    def small_back_near(full, ids):
        for k, i in zip(FAR, ids):
            recv(i, full.at[y, zlo, lax.rem(zhi + 4 - k, 4)])
        return [send(full.at[y, zlo], full.at[y, zlo], near_dev(o)) for o in NEAR]

    def small_back_y(full, ids):
        for o, i in zip(NEAR, ids):
            recv(i, full.at[y, lax.rem(zlo + 16 - o, 4)])
        return [send(full.at[y], full.at[y], y_dev(k)) for k in FAR]

    def small_done(full, ids):
        for k, i in zip(FAR, ids):
            recv(i, full.at[lax.rem(y + 4 - k, 4)])
        for t in range(50):
            i, j = t // 10, t % 10
            r, l = (8 * i, 128 * j) if j < 5 else (40 + 8 * i, 128 * j - 640)
            Xf[r : r + 8, l : l + 128] = full[t // 16, (t // 4) % 4, t % 4]

    def dp_x(buf):
        return [send(buf.at[x, c], buf.at[x, c], x_dev(k)) for k in FAR]

    def dp_core(buf, ids):
        for k, i in zip(FAR, ids):
            recv(i, buf.at[lax.rem(x + 4 - k, 4), c])
        return send(buf.at[:, c], buf.at[:, c], core_dev)

    def dp_done(buf, i):
        recv(i, buf.at[:, 1 - c])

    pr_y = small_y(PT, PRY)
    CHv = CH.reshape(4, 2, 80, 128)
    ch_x = dp_x(CHv)

    cw = cw_ref[...].astype(F32)
    row16 = rows_of((16, 4096))
    hwx[160:176, :] = jnp.where(
        row16 == 0, cw[0:1, :], jnp.where(row16 == 1, cw[1:2, :], 0.0)
    ).astype(BF16)
    hwx[176:256, :] = jnp.zeros((80, 4096), BF16)
    hw_copy.wait()

    def turn(j, _):
        at = pl.ds(pl.multiple_of(j * 128, 128), 128)
        hwxT[at, :] = jnp.transpose(hwx[:, at].astype(F32)).astype(BF16)
        return 0

    lax.fori_loop(0, 32, turn, 0)

    for k, i in zip(FAR, hid_far):
        recv(i, G.at[y, zlo, lax.rem(zhi + 4 - k, 4)])
    hid_near = [send(G.at[y, zlo], G.at[y, zlo], near_dev(o)) for o in NEAR]
    hid_y = [[send(G.at[y, zlo], G.at[y, zlo], y_dev(k)) for k in FAR]]
    pr_n = small_near(PT, PRY, pr_y, PS1, PRN)
    for o, i in zip(NEAR, hid_near):
        at = lax.rem(zlo + 16 - o, 4)
        recv(i, G.at[y, at])
        hid_y.append([send(G.at[y, at], G.at[y, at], y_dev(k)) for k in FAR])
    pr_f = small_far(PS1, PRN, pr_n, PS2, PRF)
    pr_bf = small_back_far(PS2, PRF, pr_f, PG)
    pr_bn = small_back_near(PG, pr_bf)
    pr_by = small_back_y(PG, pr_bn)
    ch_c = dp_core(CHv, ch_x)
    small_done(PG, pr_by)
    PJ[d] = Xf[...].astype(BF16)
    PJv = PJ.reshape(4, 2, 80, 640)
    pj_x = dp_x(PJv)

    left, right = Xf[0:40, :].astype(BF16), Xf[40:80, :].astype(BF16)
    log1 = dot(left, t1_ref[:, 0:640], NT) + dot(right[:, 0:384], t1_ref[:, 640:1024], NT)
    log2 = dot(right[:, 384:640], t2_ref[...], NT)
    L1s[...] = log1
    L2s[...] = log2

    def column_stats(values, goals):
        high = jnp.max(values, axis=1, keepdims=True)
        total = jnp.sum(jnp.exp(values - high), axis=1, keepdims=True)
        hit = lanes(values.shape) == goals
        return high, total, jnp.sum(jnp.where(hit, values, 0.0), axis=1, keepdims=True)

    stat1 = column_stats(log1, goal[0:40] - v * 320)
    stat2 = column_stats(log2, goal[40:80] - v * 1664)
    lane = lanes((80, 128))
    table = jnp.zeros((80, 128), F32)
    for n in range(3):
        table = jnp.where(lane == 3 + n, jnp.concatenate([stat1[n], stat2[n]], axis=0), table)
    TS[0:80, :] = table
    TS[80:128, :] = jnp.zeros((48, 128), F32)
    tail_tile = jnp.transpose(TS[...])[0:8, :]

    for n, ids in enumerate(hid_y):
        at = zlo if n == 0 else lax.rem(zlo + 16 - NEAR[n - 1], 4)
        for k, i in zip(FAR, ids):
            recv(i, G.at[lax.rem(y + 4 - k, 4), at])

    slices = []
    for k in range(1, 8):
        peer = lax.rem(d + k, 8)
        src = G.at[:, pl.ds(lax.rem(2 * peer, 4), 2), lax.div(peer, 2)]
        slices.append(send(src, HG.at[d], dp_dev(k)))

    def spread(n, _):
        zz, yy = lax.div(n, 4), lax.rem(n, 4)
        block = G.at[yy, lax.rem(zz, 4), lax.div(zz, 4)]
        base = pl.multiple_of(n * 64, 64)
        WT[pl.ds(base, 64), 0:128] = block[0:64, :]
        packed = block[64:80, :].astype(F32)
        for q in range(4):
            WT[pl.ds(pl.multiple_of(base + 16 * q, 16), 16), 128:256] = unpack_rest(packed, q)
        return 0

    lax.fori_loop(0, 64, spread, 0)

    LG[...] = dot(hwx[...], WT[...])
    words = LG[0:160, :]
    head_goal = jnp.where(cluster == 0, target, -1) - v * 160
    head_hit = rows_of((160, 256)) == head_goal
    high = jnp.max(words, axis=0, keepdims=True)
    total = jnp.sum(jnp.exp(words - high), axis=0, keepdims=True)
    picked = jnp.sum(jnp.where(head_hit, words, 0.0), axis=0, keepdims=True)
    row8 = rows_of((8, 256))
    wide_tail = jnp.concatenate([tail_tile, jnp.zeros((8, 128), F32)], axis=1)
    tile = jnp.where(
        row8 == 0, high, jnp.where(row8 == 1, total, jnp.where(row8 == 2, picked, wide_tail))
    )

    def join(slots):
        parts = [slots[i] for i in range(4)]
        result = []
        for base in (0, 3):
            m = [p[base : base + 1] for p in parts]
            top = jnp.maximum(jnp.maximum(m[0], m[1]), jnp.maximum(m[2], m[3]))
            s = [p[base + 1 : base + 2] * jnp.exp(mm - top) for p, mm in zip(parts, m)]
            t = [p[base + 2 : base + 3] for p in parts]
            result += [top, (s[0] + s[1]) + (s[2] + s[3]), (t[0] + t[1]) + (t[2] + t[3])]
        return result

    def as_tile(result):
        out = jnp.zeros((8, 256), F32)
        for n in range(6):
            out = jnp.where(row8 == n, result[n], out)
        return out

    STF[zhi] = tile
    ids = [send(STF.at[zhi], STF.at[zhi], far_dev(k)) for k in FAR]
    pj_c = dp_core(PJv, pj_x)
    for k, i in zip(FAR, ids):
        recv(i, STF.at[lax.rem(zhi + 4 - k, 4)])
    STN[zlo] = as_tile(join(STF))
    ids = [send(STN.at[zlo], STN.at[zlo], near_dev(o)) for o in NEAR]
    for o, i in zip(NEAR, ids):
        recv(i, STN.at[lax.rem(zlo + 16 - o, 4)])
    STY[y] = as_tile(join(STN))
    ids = [send(STY.at[y], STY.at[y], y_dev(k)) for k in FAR]
    for k, i in zip(FAR, ids):
        recv(i, STY.at[lax.rem(y + 4 - k, 4)])
    stats = join(STY)

    tail_lse = stats[3] + jnp.log(stats[4])
    TS[...] = jnp.zeros_like(TS)
    TS[0:1, :] = tail_lse[:, 0:128]
    TS[1:2, :] = (tail_lse - stats[5])[:, 0:128]
    columns = jnp.transpose(TS[...])[0:80, :]
    lse_col = jnp.where(live, columns[:, 0:1], 1e30)
    loss_col = columns[:, 1:2]

    def tail_gradient(values, lse, goals):
        hit = (lanes(values.shape) == goals).astype(F32)
        return (SCALE * (jnp.exp(values - lse) - hit)).astype(BF16)

    own1 = tail_gradient(L1s[...], lse_col[0:40], goal[0:40] - v * 320)
    own2 = tail_gradient(L2s[...], lse_col[40:80], jnp.where(live, goal, -(1 << 20))[40:80] - v * 1664)
    back1 = dot(own1, t1_ref[...])
    back2 = dot(own2, t2_ref[...])
    to_tiles(BT, back1, back2)
    bk_y = small_y(BT, BRY)

    INF[d] = jnp.where(lane == 0, lse_col, jnp.where(lane == 1, goal.astype(F32), 0.0))
    INFv = INF.reshape(4, 2, 80, 128)
    inf_x = dp_x(INFv)

    entry0, entry1 = LG[160:161, :], LG[161:162, :]
    top = jnp.maximum(stats[0], jnp.maximum(entry0, entry1))
    summed = stats[1] * jnp.exp(stats[0] - top) + (jnp.exp(entry0 - top) + jnp.exp(entry1 - top))
    lse = top + jnp.log(summed)
    is1, is2 = (cluster == 1).astype(F32), (cluster == 2).astype(F32)
    chosen_logit = stats[2] + (is1 * entry0 + is2 * entry1)
    tail_loss = jnp.sum(jnp.where(slot_hit, loss_col, 0.0), axis=0, keepdims=True)
    loss_ref[...] = (lse - chosen_logit) + tail_loss

    inside = lanes((160, 256)) < 160
    grad = jnp.where(inside, SCALE * (jnp.exp(LG[0:160, :] - lse) - head_hit.astype(F32)), 0.0)
    inside1 = lanes((1, 256)) < 160
    ge0 = jnp.where(inside1, SCALE * (jnp.exp(entry0 - lse) - is1), 0.0)
    ge1 = jnp.where(inside1, SCALE * (jnp.exp(entry1 - lse) - is2), 0.0)
    GP[d, 0:160, :] = grad[:, 0:128].astype(BF16)
    rounded_rest = grad[:, 128:256]
    GP[d, 160:208, :] = pack_rest(rounded_rest, 48).astype(BF16)
    GPv = GP.reshape(4, 2, 208, 128)
    gp_x = dp_x(GPv)

    row96 = rows_of((96, 256))
    mine = (v == 0).astype(F32)
    low = jnp.where(row96 == 0, ge0 * mine, jnp.where(row96 == 1, ge1 * mine, 0.0))
    grad_ext = jnp.concatenate([grad, low], axis=0).astype(BF16)

    def part(n, _):
        zz = lax.rem(n, 16)
        at = pl.ds(pl.multiple_of(zz * 256, 256), 256)
        product = dot(hwxT[at, :], grad_ext)
        for yy in range(4):
            block = GB.at[yy, lax.rem(zz, 4), lax.div(zz, 4)]
            piece = product[64 * yy : 64 * yy + 64]
            block[0:64, :] = piece[:, 0:128].astype(BF16)
            block[64:80, :] = pack_rest(piece[:, 128:256], 16).astype(BF16)
        return 0

    lax.fori_loop(0, 16, part, 0)
    gh_y = []
    for o in NEAR + (0,):
        at = lax.rem(zlo + o, 4)
        gh_y.append(
            [
                send(GB.at[lax.rem(y + k, 4), at], GRY.at[k - 1, at], y_dev(k))
                for k in FAR
            ]
        )

    bk_n = small_near(BT, BRY, bk_y, BS1, BRN)
    entries = jnp.where(rows_of((8, 256)) % 2 == 0, ge0, ge1).astype(BF16)
    full = dot(entries, WT[...], NT)
    pair = lax.div(rows_of((8, 1024)), 2)
    packed_cl = jnp.zeros((8, 1024), F32)
    for k in range(4):
        packed_cl = jnp.where(pair == k, full[:, 1024 * k : 1024 * k + 1024], packed_cl)
    GC[d] = packed_cl
    GCv = GC.reshape(4, 2, 8, 1024)
    gc_x = dp_x(GCv)

    bk_f = small_far(BS1, BRN, bk_n, BS2, BRF)
    bk_bf = small_back_far(BS2, BRF, bk_f, BG)

    inf_c = dp_core(INFv, inf_x)
    gp_c = dp_core(GPv, gp_x)
    bk_bn = small_back_near(BG, bk_bf)

    gh_n = []
    for n, o in enumerate(NEAR):
        at = lax.rem(zlo + o, 4)
        for k, i in zip(FAR, gh_y[n]):
            recv(i, GRY.at[k - 1, at])
        GS1[n] = (
            (GB[y, at].astype(F32) + GRY[0, at].astype(F32))
            + (GRY[1, at].astype(F32) + GRY[2, at].astype(F32))
        ).astype(BF16)
        gh_n.append(send(GS1.at[n], GRN.at[n], near_dev(o)))
        if n == 0:
            bk_by = small_back_y(BG, bk_bn)
    gc_c = dp_core(GCv, gc_x)
    small_done(BG, bk_by)
    BK[d] = Xf[...].astype(BF16)
    BKv = BK.reshape(4, 2, 80, 640)
    bk_x = dp_x(BKv)

    for k, i in zip(FAR, gh_y[3]):
        recv(i, GRY.at[k - 1, zlo])
    mine_sum = (GB[y, zlo].astype(F32) + GRY[0, zlo].astype(F32)) + (
        GRY[1, zlo].astype(F32) + GRY[2, zlo].astype(F32)
    )
    for n, i in enumerate(gh_n):
        recv(i, GRN.at[n])
    GS2[...] = mine_sum + (
        GRN[0].astype(F32) + (GRN[1].astype(F32) + GRN[2].astype(F32))
    )
    GRF[3] = GS2[zhi].astype(BF16)
    for k in FAR:
        GRF[3 + k] = GS2[lax.rem(zhi + k, 4)].astype(BF16)
    gh_f = [send(GRF.at[3 + k], GRF.at[k - 1], far_dev(k)) for k in FAR]

    def assemble(src, dst1, dst2):
        for g in range(8):
            both = src[g].astype(F32)
            dst1[40 * g : 40 * g + 40, 0:640] = both[0:40, :]
            dst1[40 * g : 40 * g + 40, 640:1024] = both[40:80, 0:384]
            dst2[40 * g : 40 * g + 40, :] = both[40:80, 384:640]

    dp_done(PJv, pj_c)
    dp_done(INFv, inf_c)
    assemble(PJ, P1f, P2f)
    P1b[...] = P1f[...].astype(BF16)
    P2b[...] = P2f[...].astype(BF16)

    def gather_column(lo, lane_at):
        return jnp.concatenate([INF[g, lo : lo + 40, lane_at : lane_at + 1] for g in range(8)], axis=0)

    lse1, goal1 = gather_column(0, 0), gather_column(0, 1).astype(jnp.int32)
    all1 = dot(P1b[...], t1_ref[...], NT)
    base1 = jnp.where(goal1 < 0, -(1 << 20), goal1 - v * 320)
    grad1 = tail_gradient(all1, lse1, base1)
    gt1_ref[...] = dot(grad1, P1b[:, pl.ds(pl.multiple_of(d * 128, 128), 128)], TN)

    lse2, goal2 = gather_column(40, 0), gather_column(40, 1).astype(jnp.int32)
    base2 = jnp.where(goal2 < 0, -(1 << 20), goal2 - v * 1664)
    select = jnp.where(lanes((32, 256)) == rows_of((32, 256)) + d * 32, 1.0, 0.0).astype(BF16)
    mine2 = dot(select, P2b[...], NT).astype(BF16)
    P1f[:, 0:128] = jnp.broadcast_to(lse2, (320, 128))
    P1f[:, 128:256] = jnp.broadcast_to(base2.astype(F32), (320, 128))

    def tail_two(j, _):
        at = pl.multiple_of(j * 128, 128)
        logits = dot(P2b[...], t2_ref[pl.ds(at, 128), :], NT)
        hit = (lanes((320, 128)).astype(F32) + (j * 128).astype(F32)) == P1f[:, 128:256]
        grads = (SCALE * (jnp.exp(logits - P1f[:, 0:128]) - hit.astype(F32))).astype(BF16)
        gt2_ref[:, pl.ds(at, 128)] = dot(mine2, grads)
        return 0

    lax.fori_loop(0, 13, tail_two, 0)
    bk_c = dp_core(BKv, bk_x)

    HG[d] = G[:, pl.ds(lax.rem(2 * d, 4), 2), lax.div(d, 2)]
    dp_done(GPv, gp_c)
    for k, i in zip(range(1, 8), slices):
        recv(i, HG.at[lax.rem(d + 8 - k, 8)])
    head_ref[...] = jnp.zeros_like(head_ref)

    def head_group(g, _):
        GU[:, 0:128] = GP[g, 0:160, :]
        rest = GP[g, 160:208, :].astype(F32)
        for q in range(4):
            rows = 48 if q < 3 else 16
            GU[48 * q : 48 * q + rows, 128:256] = unpack_rest(rest[0:rows], q)
        for b in range(8):
            block = HG.at[g, b % 4, b // 4]
            HU[64 * b : 64 * b + 64, 0:128] = block[0:64, :]
            packed = block[64:80, :].astype(F32)
            for q in range(4):
                HU[64 * b + 16 * q : 64 * b + 16 * q + 16, 128:256] = unpack_rest(packed, q)
        head_ref[...] += dot(GU[...], HU[...], NT)
        return 0

    lax.fori_loop(0, 8, head_group, 0)

    dp_done(GCv, gc_c)
    cl_ref[...] = ((GC[0] + GC[1]) + (GC[2] + GC[3])) + ((GC[4] + GC[5]) + (GC[6] + GC[7]))

    both = BK[d].astype(F32)
    b1a, b1b = both[0:40, :].astype(BF16), both[40:80, 0:384].astype(BF16)
    b2 = both[40:80, 384:640].astype(BF16)
    hot1 = jnp.where(slot_hit[0:40], 1.0, 0.0)
    hot2 = jnp.where(slot_hit[40:80], 1.0, 0.0)
    back_one = dot(p1_ref[:, 0:640], b1a, NT) + dot(p1_ref[:, 640:1024], b1b, NT)
    add = dot_exact(back_one, hot1) + dot_exact(dot(p2_ref[...], b2, NT), hot2)
    for n, i in enumerate(gh_f):
        recv(i, GRF.at[n])
    block = GS2[zhi] + (GRF[0].astype(F32) + (GRF[1].astype(F32) + GRF[2].astype(F32)))
    hp[:, 0:128] = block[0:64, :]
    for q in range(4):
        part_q = block[64:80, :]
        hp[16 * q : 16 * q + 16, 128:256] = part_q if q == 0 else pltpu.roll(part_q, 128 - 32 * q, 1)
    gh_ref[...] = (hp[...] + add)[:, 0:160]

    dp_done(CHv, ch_c)
    dp_done(BKv, bk_c)
    assemble(BK, P1f, P2f)
    for g in range(8):
        rows_g = CH[g].astype(F32)
        C1f[40 * g : 40 * g + 40, :] = rows_g[0:40, :]
        C2f[40 * g : 40 * g + 40, :] = rows_g[40:80, :]
    gp1_ref[...] = dot(C1f[...].astype(BF16), P1f[...].astype(BF16), TN)[0:64, :]
    gp2_ref[...] = dot(C2f[...].astype(BF16), P2f[...].astype(BF16), TN)[0:64, :]

    for copy in sent:
        copy.wait_send()


def on_device(
    hidden_states, head_weight, cluster_weight, proj_one, tail_one, proj_two, tail_two,
    targets, token_cluster, tail_rows, tail_counts,
):
    slot = jnp.arange(40, dtype=jnp.int32)[None, :]
    rows = jnp.where(slot < tail_counts[0][:, None], tail_rows[0], -1).reshape(1, 80)
    meta = jnp.concatenate(
        [
            jnp.pad(jnp.stack([targets, token_cluster]), ((0, 6), (0, 96)), constant_values=-1),
            jnp.pad(rows, ((0, 7), (0, 48)), constant_values=-1),
        ],
        axis=1,
    )
    vmem = pl.BlockSpec(memory_space=pltpu.VMEM)
    shapes = [
        ((1, 256), F32), ((64, 160), F32), ((160, 512), F32), ((8, 1024), F32),
        ((64, 1024), F32), ((320, 128), F32), ((64, 256), F32), ((32, 1664), F32),
    ]
    V = pltpu.VMEM
    scratch = [
        V((64, 256), F32), V((4, 4, 4, 80, 128), BF16), V((4096, 256), BF16), V((256, 4096), BF16),
        V((4096, 256), BF16), V((8, 4, 2, 80, 128), BF16), V((512, 256), BF16),
        V((8, 80, 128), BF16), V((4, 4, 4, 8, 128), F32), V((3, 4, 4, 8, 128), F32),
        V((3, 4, 8, 128), F32), V((3, 8, 128), F32), V((4, 4, 8, 128), F32), V((4, 8, 128), F32),
        V((4, 4, 4, 8, 128), F32), V((80, 640), F32), V((8, 80, 640), BF16),
        V((320, 1024), F32), V((320, 256), F32), V((320, 1024), BF16), V((320, 256), BF16),
        V((8, 256), F32), V((4, 8, 256), F32), V((4, 8, 256), F32), V((4, 8, 256), F32), V((128, 128), F32),
        V((256, 256), F32), V((40, 320), F32), V((40, 1664), F32), V((8, 80, 128), F32),
        V((8, 208, 128), BF16), V((160, 256), BF16), V((8, 8, 1024), F32),
        V((4, 4, 4, 8, 128), F32), V((3, 4, 4, 8, 128), F32), V((3, 4, 8, 128), F32), V((3, 8, 128), F32),
        V((4, 4, 8, 128), F32), V((4, 8, 128), F32), V((4, 4, 4, 8, 128), F32), V((8, 80, 640), BF16),
        V((320, 128), F32), V((320, 128), F32),
        V((4, 4, 4, 80, 128), BF16), V((3, 4, 4, 80, 128), BF16), V((3, 4, 80, 128), BF16),
        V((3, 4, 80, 128), BF16), V((4, 80, 128), F32), V((7, 80, 128), BF16),
        pltpu.SemaphoreType.DMA((SEMS,)), pltpu.SemaphoreType.DMA((SEMS,)), pltpu.SemaphoreType.DMA,
    ]
    out = pl.pallas_call(
        kernel,
        out_shape=[jax.ShapeDtypeStruct(s, t) for s, t in shapes],
        in_specs=[vmem, pl.BlockSpec(memory_space=pl.ANY)] + [vmem] * 6,
        out_specs=[vmem] * 8,
        scratch_shapes=scratch,
        compiler_params=pltpu.CompilerParams(
            collective_id=0, has_side_effects=True, vmem_limit_bytes=56 * 1024 * 1024
        ),
    )(
        hidden_states.T, head_weight, cluster_weight, proj_one, tail_one, proj_two, tail_two, meta
    )
    loss, gh, head, cl, gp1, gt1, gp2, gt2 = out
    return (
        loss[0, :160],
        gh.T,
        head,
        cl.reshape(4, 2, 1024).transpose(1, 0, 2).reshape(2, 4096),
        gp1,
        gt1,
        gp2,
        gt2.T,
    )


def solution(mesh):
    return jax.shard_map(
        on_device,
        mesh=mesh,
        in_specs=(
            P("dp", "vocab"), P("vocab", None), P(), P("vocab", None), P("vocab", None),
            P("vocab", None), P("vocab", None), P("dp"), P("dp"), P("dp", None, None), P("dp", None),
        ),
        out_specs=(
            P("dp"), P("dp", "vocab"), P("vocab", "dp"), P(), P("vocab", None),
            P("vocab", "dp"), P("vocab", None), P("vocab", "dp"),
        ),
        check_vma=False,
    )
```

time: 1290 us -> 137 us (0.11)
  blocking collectives: 918 us -> 0 us
  waiting for transfers between devices: 172 us -> 0 us
  Pallas kernels: 0 us -> 123 us
  local copies, waits for them, and re-layouts: 123 us -> 10.4 us
  other arithmetic: 22.5 us -> 2.04 us
  matrix products: 20.3 us -> 0 us
  between operations: 15.6 us -> 0.67 us
    unnamed x2 -> x0, blocking collectives: 442 us -> none
    psum x2 -> x0, blocking collectives: 255 us -> none  [the longest x1 232 us: on_device(): projected_sums = lax.psum((partial_sums[0], partial_sums[1]), 'vocab')]
    all_gather x3 -> x0, blocking collectives: 221 us -> none  [the longest x1 194 us: on_device(): lax.all_gather(grad_list[0], 'dp', axis=0, tiled=True)]
    pallas_call x0 -> x1, Pallas kernels: none -> 123 us  [on_device(): pl.pallas_call(kernel, out_shape=[jax.ShapeDtypeStruct(s, t) for s, t in...]
    dynamic_slice x128 -> x0, local copies, waits for them, and re-layouts: 88.8 us -> none  [the longest x126 88.7 us: joined(): lax.scan(lambda total, slab: (join(total, slab), None), head, tail)]
    psum x1 -> x0, waiting for transfers between devices: 72.8 us -> none  [on_device(): small_grads = lax.psum((proj_parts[0], proj_parts[1], entry_part), 'dp')]
    all_gather x3 -> x0, waiting for transfers between devices: 54.2 us -> none  [the longest x1 54.1 us: on_device(): lax.all_gather(head_grad, 'vocab', axis=1, tiled=True)]
    reduce_scatter x1 -> x0, waiting for transfers between devices: 44.6 us -> none  [on_device(): lax.psum_scatter(head_part, 'dp', scatter_dimension=1, tiled=True)]
  transfers between devices with their start and end apart: 6 -> 0, of which waited for: 3 -> 0; matrix products, arithmetic and copies ran while one was open for 12% -> 0% of each run, Pallas kernels for 0% -> 0%
where the time goes in v1:
time: 137 us
  Pallas kernels  123 us (90%)
  local copies, waits for them, and re-layouts  10.4 us (8%)
  other arithmetic  2.04 us (1%)
    pallas_call x1, Pallas kernels, on_device(): pl.pallas_call(kernel, out_shape=[jax.ShapeDtypeStruct(s, t) for s, t in...  123 us
    unnamed x13, local copies, waits for them, and re-layouts  8.07 us

profile of v1, /device:TPU:1, one launch (start us, length us, event | category | flops | bytes accessed | tf_op | source)
XLA Modules:
  0.0 136.5 jit_solution(103785203600260341)
XLA Ops:
  0.6 0.8 squeeze.6
  1.4 0.7 iota_compare_fusion.2
  2.1 0.1 lt.29
  2.2 0.7 pad_add_fusion
  2.9 0.6 select_add_fusion.meta_ref
  3.5 123.5 %shard_map.170 = (f32[1,256]{1,0:T(1,128)}, f32[64,160]{1,0:T(8,128)}, f32[160,512]{1,0:T(8,128)}, f32[8,1024]{1,0:T(8,128)}, f32[64,1024]{1,0:T(8,128)}, /*inde...) custom-call(bf16[64,160]{1,0:T(8,128)(2,1)} %bitcast.13, bf16[160,4096]{1,0:T(8,128)(2,1)} %hw_ref.1, ...), custom_call_target="tpu_custom_call" | custom-call | tf_op jit(solution)/shard_map/pallas_call | solution.py:604
  127.0 0.0 copy-start.1
  127.0 0.0 copy-start.2
  127.0 0.0 copy-start
  127.0 1.4 %reshape.56 = f32[4,2,1024]{2,1,0:T(2,128)} reshape(f32[8,1024]{1,0:T(8,128)} %get-tuple-element.19) | data formatting | bytes 65536 | tf_op jit(solution)/shard_map/reshape | solution.py:621
  128.5 1.2 copy.27
  129.7 1.5 %copy.28 = f32[160,64]{0,1:T(8,128)} copy(f32[160,64]{0,1:T(8,128)} %bitcast.12) | data formatting | bytes 81920
  131.2 1.7 %copy.29 = f32[160,512]{1,0:T(8,128)} copy(f32[160,512]{1,0:T(8,128)} %get-tuple-element.34) | data formatting | bytes 655360
  132.9 1.7 %copy.30 = f32[64,1024]{1,0:T(8,128)} copy(f32[64,1024]{1,0:T(8,128)} %get-tuple-element.36) | data formatting | bytes 524288
  134.6 0.0 copy-done.1
  134.6 0.7 copy.31
  135.2 0.0 copy-done.2
  135.2 0.6 copy.32
  135.9 0.0 copy-done
  135.9 0.7 copy.33
  (1 shorter events, 0.0 us)
Async XLA Ops:
  127.0 7.6 %copy-start.1 = (f32[320,128]{1,0:T(8,128)S(1)}, f32[320,128]{1,0:T(8,128)}, u32[]{:S(2)}) copy-start(f32[320,128]{1,0:T(8,128)} %get-tuple-element.37) | copy-start | bytes 491524
  127.0 8.2 %copy-start.2 = (f32[64,256]{1,0:T(8,128)S(1)}, f32[64,256]{1,0:T(8,128)}, u32[]{:S(2)}) copy-start(f32[64,256]{1,0:T(8,128)} %get-tuple-element.38) | copy-start | bytes 196612
  127.0 8.8 %copy-start = (f32[32,1664]{1,0:T(8,128)S(1)}, f32[32,1664]{1,0:T(8,128)}, u32[]{:S(2)}) copy-start(f32[32,1664]{1,0:T(8,128)} %get-tuple-element.23) | copy-start | bytes 638980

commit v2 on v1

--- a/solution.py
+++ b/solution.py
@@ -54,16 +54,16 @@
 
 
 def kernel(
-    hid_ref, hw_ref, cw_ref, p1_ref, t1_ref, p2_ref, t2_ref, meta_ref,
+    hid_ref, hw_ref, cw_ref, p1_ref, t1_hbm, p2_ref, t2_hbm, tgt_ref, clu_ref, rows_ref, count_ref,
     loss_ref, gh_ref, head_ref, cl_ref, gp1_ref, gt1_ref, gp2_ref, gt2_ref,
-    hp, G, WT, hwx, hwxT, HG, HU,
+    t1_ref, t2_ref, ids, hp, G, WT, hwx, hwxT, HG, HU,
     CH, PT, PRY, PRN, PRF, PS1, PS2, PG, Xf, PJ,
     P1f, P2f, P1b, P2b,
     ST, STF, STN, STY, TS,
     LG, L1s, L2s, INF, GP, GU, GC,
     BT, BRY, BRN, BRF, BS1, BS2, BG, BK, C1f, C2f,
     GB, GRY, GS1, GRN, GS2, GRF,
-    ssem, rsem, lsem,
+    ssem, rsem, lsem, tsem,
 ):
     d = lax.axis_index("dp")
     v = lax.axis_index("vocab")
@@ -109,7 +109,11 @@
         ).wait_recv()
 
     hw_copy = pltpu.make_async_copy(hw_ref, hwx.at[0:160], lsem)
+    t1_copy = pltpu.make_async_copy(t1_hbm, t1_ref, tsem.at[0])
+    t2_copy = pltpu.make_async_copy(t2_hbm, t2_ref, tsem.at[1])
     hw_copy.start()
+    t1_copy.start()
+    t2_copy.start()
 
     barrier = pltpu.get_barrier_semaphore()
     greeted = 0
@@ -130,10 +134,18 @@
     G[y, zlo, zhi, 64:80, :] = pack_rest(hp[:, 128:256], 16).astype(BF16)
 
     TS[...] = jnp.zeros_like(TS)
-    TS[0:8, :] = meta_ref[:, 256:384].astype(F32)
-    row_col = jnp.transpose(TS[...])[0:80, 0:1].astype(jnp.int32)
-    target = meta_ref[0:1, 0:256]
-    cluster = meta_ref[1:2, 0:256]
+    lane40 = lanes((1, 40))
+    for n in range(2):
+        TS[n : n + 1, 0:40] = jnp.where(
+            lane40 < count_ref[0:1, n : n + 1], rows_ref[n : n + 1, :], -1
+        ).astype(F32)
+    turned = jnp.transpose(TS[...])
+    row_col = jnp.concatenate([turned[0:40, 0:1], turned[0:40, 1:2]], axis=0).astype(jnp.int32)
+    ids[...] = jnp.full((2, 256), -1, jnp.int32)
+    ids[0:1, 0:160] = tgt_ref[...]
+    ids[1:2, 0:160] = clu_ref[...]
+    target = ids[0:1, :]
+    cluster = ids[1:2, :]
     slot_hit = lanes((80, 256)) == row_col
     onehot = jnp.where(slot_hit, 1.0, 0.0).astype(BF16)
     live = row_col >= 0
@@ -185,7 +197,23 @@
             send(sums2.at[lax.rem(zhi + k, 4)], fslots.at[k - 1], far_dev(k)) for k in FAR
         ]
 
-    def small_back_far(sums2, fslots, ids, full):
+    def small_sum_y(sums2, fslots, ids, full):
+        for n, i in enumerate(ids):
+            recv(i, fslots.at[n])
+        full[y, zlo, zhi] = (sums2[zhi] + fslots[0]) + (fslots[1] + fslots[2])
+        return [send(full.at[y, zlo, zhi], full.at[y, zlo, zhi], y_dev(k)) for k in FAR]
+
+    def small_spread_far(full, ids):
+        for k, i in zip(FAR, ids):
+            recv(i, full.at[lax.rem(y + 4 - k, 4), zlo, zhi])
+        return [send(full.at[:, zlo, zhi], full.at[:, zlo, zhi], far_dev(k)) for k in FAR]
+
+    def small_spread_near(full, ids):
+        for k, i in zip(FAR, ids):
+            recv(i, full.at[:, zlo, lax.rem(zhi + 4 - k, 4)])
+        return [send(full.at[:, zlo], full.at[:, zlo], near_dev(o)) for o in NEAR]
+
+    def small_sum_far(sums2, fslots, ids, full):
         for n, i in enumerate(ids):
             recv(i, fslots.at[n])
         full[y, zlo, zhi] = (sums2[zhi] + fslots[0]) + (fslots[1] + fslots[2])
@@ -201,9 +229,9 @@
             recv(i, full.at[y, lax.rem(zlo + 16 - o, 4)])
         return [send(full.at[y], full.at[y], y_dev(k)) for k in FAR]
 
-    def small_done(full, ids):
-        for k, i in zip(FAR, ids):
-            recv(i, full.at[lax.rem(y + 4 - k, 4)])
+    def small_done(full, waits):
+        for i, yy, zl in waits:
+            recv(i, full.at[yy] if zl is None else full.at[yy, zl])
         for t in range(50):
             i, j = t // 10, t % 10
             r, l = (8 * i, 128 * j) if j < 5 else (40 + 8 * i, 128 * j - 640)
@@ -234,30 +262,45 @@
 
     def turn(j, _):
         at = pl.ds(pl.multiple_of(j * 128, 128), 128)
-        hwxT[at, :] = jnp.transpose(hwx[:, at].astype(F32)).astype(BF16)
+        hwxT[at, :] = jnp.transpose(hwx[:, at])
         return 0
 
-    lax.fori_loop(0, 32, turn, 0)
-
+    def spread(yy, zl):
+        for zh in range(4):
+            block = G.at[yy, zl, zh]
+            base = pl.multiple_of(((zh * 4 + zl) * 4 + yy) * 64, 64)
+            WT[pl.ds(base, 64), 0:128] = block[0:64, :]
+            packed = block[64:80, :].astype(F32)
+            for q in range(4):
+                WT[pl.ds(pl.multiple_of(base + 16 * q, 16), 16), 128:256] = unpack_rest(packed, q)
+
+    pr_n = small_near(PT, PRY, pr_y, PS1, PRN)
+    lax.fori_loop(0, 8, turn, 0)
     for k, i in zip(FAR, hid_far):
         recv(i, G.at[y, zlo, lax.rem(zhi + 4 - k, 4)])
     hid_near = [send(G.at[y, zlo], G.at[y, zlo], near_dev(o)) for o in NEAR]
+    pr_f = small_far(PS1, PRN, pr_n, PS2, PRF)
     hid_y = [[send(G.at[y, zlo], G.at[y, zlo], y_dev(k)) for k in FAR]]
-    pr_n = small_near(PT, PRY, pr_y, PS1, PRN)
+    lax.fori_loop(8, 16, turn, 0)
+    pr_by = small_sum_y(PS2, PRF, pr_f, PG)
     for o, i in zip(NEAR, hid_near):
         at = lax.rem(zlo + 16 - o, 4)
         recv(i, G.at[y, at])
         hid_y.append([send(G.at[y, at], G.at[y, at], y_dev(k)) for k in FAR])
-    pr_f = small_far(PS1, PRN, pr_n, PS2, PRF)
-    pr_bf = small_back_far(PS2, PRF, pr_f, PG)
-    pr_bn = small_back_near(PG, pr_bf)
-    pr_by = small_back_y(PG, pr_bn)
+    pr_bf = small_spread_far(PG, pr_by)
+    lax.fori_loop(16, 24, turn, 0)
+    pr_bn = small_spread_near(PG, pr_bf)
     ch_c = dp_core(CHv, ch_x)
-    small_done(PG, pr_by)
+    lax.fori_loop(24, 32, turn, 0)
+    for zl in range(4):
+        spread(y, zl)
+    small_done(PG, [(i, slice(None), lax.rem(zlo + 16 - o, 4)) for o, i in zip(NEAR, pr_bn)])
     PJ[d] = Xf[...].astype(BF16)
     PJv = PJ.reshape(4, 2, 80, 640)
     pj_x = dp_x(PJv)
 
+    t1_copy.wait()
+    t2_copy.wait()
     left, right = Xf[0:40, :].astype(BF16), Xf[40:80, :].astype(BF16)
     log1 = dot(left, t1_ref[:, 0:640], NT) + dot(right[:, 0:384], t1_ref[:, 640:1024], NT)
     log2 = dot(right[:, 384:640], t2_ref[...], NT)
@@ -280,28 +323,18 @@
     TS[80:128, :] = jnp.zeros((48, 128), F32)
     tail_tile = jnp.transpose(TS[...])[0:8, :]
 
-    for n, ids in enumerate(hid_y):
+    for n, ids_y in enumerate(hid_y):
         at = zlo if n == 0 else lax.rem(zlo + 16 - NEAR[n - 1], 4)
-        for k, i in zip(FAR, ids):
-            recv(i, G.at[lax.rem(y + 4 - k, 4), at])
+        for k, i in zip(FAR, ids_y):
+            yy = lax.rem(y + 4 - k, 4)
+            recv(i, G.at[yy, at])
+            spread(yy, at)
 
     slices = []
     for k in range(1, 8):
         peer = lax.rem(d + k, 8)
         src = G.at[:, pl.ds(lax.rem(2 * peer, 4), 2), lax.div(peer, 2)]
         slices.append(send(src, HG.at[d], dp_dev(k)))
-
-    def spread(n, _):
-        zz, yy = lax.div(n, 4), lax.rem(n, 4)
-        block = G.at[yy, lax.rem(zz, 4), lax.div(zz, 4)]
-        base = pl.multiple_of(n * 64, 64)
-        WT[pl.ds(base, 64), 0:128] = block[0:64, :]
-        packed = block[64:80, :].astype(F32)
-        for q in range(4):
-            WT[pl.ds(pl.multiple_of(base + 16 * q, 16), 16), 128:256] = unpack_rest(packed, q)
-        return 0
-
-    lax.fori_loop(0, 64, spread, 0)
 
     LG[...] = dot(hwx[...], WT[...])
     words = LG[0:160, :]
@@ -334,17 +367,17 @@
         return out
 
     STF[zhi] = tile
-    ids = [send(STF.at[zhi], STF.at[zhi], far_dev(k)) for k in FAR]
+    near_ids = [send(STF.at[zhi], STF.at[zhi], far_dev(k)) for k in FAR]
     pj_c = dp_core(PJv, pj_x)
-    for k, i in zip(FAR, ids):
+    for k, i in zip(FAR, near_ids):
         recv(i, STF.at[lax.rem(zhi + 4 - k, 4)])
     STN[zlo] = as_tile(join(STF))
-    ids = [send(STN.at[zlo], STN.at[zlo], near_dev(o)) for o in NEAR]
-    for o, i in zip(NEAR, ids):
+    near_ids = [send(STN.at[zlo], STN.at[zlo], near_dev(o)) for o in NEAR]
+    for o, i in zip(NEAR, near_ids):
         recv(i, STN.at[lax.rem(zlo + 16 - o, 4)])
     STY[y] = as_tile(join(STN))
-    ids = [send(STY.at[y], STY.at[y], y_dev(k)) for k in FAR]
-    for k, i in zip(FAR, ids):
+    near_ids = [send(STY.at[y], STY.at[y], y_dev(k)) for k in FAR]
+    for k, i in zip(FAR, near_ids):
         recv(i, STY.at[lax.rem(y + 4 - k, 4)])
     stats = join(STY)
 
@@ -378,7 +411,7 @@
     is1, is2 = (cluster == 1).astype(F32), (cluster == 2).astype(F32)
     chosen_logit = stats[2] + (is1 * entry0 + is2 * entry1)
     tail_loss = jnp.sum(jnp.where(slot_hit, loss_col, 0.0), axis=0, keepdims=True)
-    loss_ref[...] = (lse - chosen_logit) + tail_loss
+    loss_ref[...] = ((lse - chosen_logit) + tail_loss)[:, 0:160]
 
     inside = lanes((160, 256)) < 160
     grad = jnp.where(inside, SCALE * (jnp.exp(LG[0:160, :] - lse) - head_hit.astype(F32)), 0.0)
@@ -396,29 +429,28 @@
     low = jnp.where(row96 == 0, ge0 * mine, jnp.where(row96 == 1, ge1 * mine, 0.0))
     grad_ext = jnp.concatenate([grad, low], axis=0).astype(BF16)
 
-    def part(n, _):
-        zz = lax.rem(n, 16)
-        at = pl.ds(pl.multiple_of(zz * 256, 256), 256)
-        product = dot(hwxT[at, :], grad_ext)
-        for yy in range(4):
-            block = GB.at[yy, lax.rem(zz, 4), lax.div(zz, 4)]
-            piece = product[64 * yy : 64 * yy + 64]
-            block[0:64, :] = piece[:, 0:128].astype(BF16)
-            block[64:80, :] = pack_rest(piece[:, 128:256], 16).astype(BF16)
-        return 0
-
-    lax.fori_loop(0, 16, part, 0)
     gh_y = []
-    for o in NEAR + (0,):
+
+    def part(o):
         at = lax.rem(zlo + o, 4)
+        for zh in range(4):
+            rows = pl.ds(pl.multiple_of((zh * 4 + at) * 256, 256), 256)
+            product = dot(hwxT[rows, :], grad_ext)
+            for yy in range(4):
+                block = GB.at[yy, at, zh]
+                piece = product[64 * yy : 64 * yy + 64]
+                block[0:64, :] = piece[:, 0:128].astype(BF16)
+                block[64:80, :] = pack_rest(piece[:, 128:256], 16).astype(BF16)
         gh_y.append(
-            [
-                send(GB.at[lax.rem(y + k, 4), at], GRY.at[k - 1, at], y_dev(k))
-                for k in FAR
-            ]
+            [send(GB.at[lax.rem(y + k, 4), at], GRY.at[k - 1, at], y_dev(k)) for k in FAR]
         )
 
+    part(NEAR[0])
     bk_n = small_near(BT, BRY, bk_y, BS1, BRN)
+    part(NEAR[1])
+    part(NEAR[2])
+    bk_f = small_far(BS1, BRN, bk_n, BS2, BRF)
+    part(0)
     entries = jnp.where(rows_of((8, 256)) % 2 == 0, ge0, ge1).astype(BF16)
     full = dot(entries, WT[...], NT)
     pair = lax.div(rows_of((8, 1024)), 2)
@@ -428,32 +460,28 @@
     GC[d] = packed_cl
     GCv = GC.reshape(4, 2, 8, 1024)
     gc_x = dp_x(GCv)
-
-    bk_f = small_far(BS1, BRN, bk_n, BS2, BRF)
-    bk_bf = small_back_far(BS2, BRF, bk_f, BG)
-
+    bk_bf = small_sum_far(BS2, BRF, bk_f, BG)
     inf_c = dp_core(INFv, inf_x)
     gp_c = dp_core(GPv, gp_x)
-    bk_bn = small_back_near(BG, bk_bf)
 
     gh_n = []
-    for n, o in enumerate(NEAR):
-        at = lax.rem(zlo + o, 4)
+
+    def chunk_near(n):
+        at = lax.rem(zlo + NEAR[n], 4)
         for k, i in zip(FAR, gh_y[n]):
             recv(i, GRY.at[k - 1, at])
         GS1[n] = (
             (GB[y, at].astype(F32) + GRY[0, at].astype(F32))
             + (GRY[1, at].astype(F32) + GRY[2, at].astype(F32))
         ).astype(BF16)
-        gh_n.append(send(GS1.at[n], GRN.at[n], near_dev(o)))
-        if n == 0:
-            bk_by = small_back_y(BG, bk_bn)
+        gh_n.append(send(GS1.at[n], GRN.at[n], near_dev(NEAR[n])))
+
+    chunk_near(0)
+    bk_bn = small_back_near(BG, bk_bf)
+    chunk_near(1)
+    bk_by = small_back_y(BG, bk_bn)
+    chunk_near(2)
     gc_c = dp_core(GCv, gc_x)
-    small_done(BG, bk_by)
-    BK[d] = Xf[...].astype(BF16)
-    BKv = BK.reshape(4, 2, 80, 640)
-    bk_x = dp_x(BKv)
-
     for k, i in zip(FAR, gh_y[3]):
         recv(i, GRY.at[k - 1, zlo])
     mine_sum = (GB[y, zlo].astype(F32) + GRY[0, zlo].astype(F32)) + (
@@ -464,10 +492,13 @@
     GS2[...] = mine_sum + (
         GRN[0].astype(F32) + (GRN[1].astype(F32) + GRN[2].astype(F32))
     )
-    GRF[3] = GS2[zhi].astype(BF16)
     for k in FAR:
-        GRF[3 + k] = GS2[lax.rem(zhi + k, 4)].astype(BF16)
-    gh_f = [send(GRF.at[3 + k], GRF.at[k - 1], far_dev(k)) for k in FAR]
+        GRF[2 + k] = GS2[lax.rem(zhi + k, 4)].astype(BF16)
+    gh_f = [send(GRF.at[2 + k], GRF.at[k - 1], far_dev(k)) for k in FAR]
+    small_done(BG, [(i, lax.rem(y + 4 - k, 4), None) for k, i in zip(FAR, bk_by)])
+    BK[d] = Xf[...].astype(BF16)
+    BKv = BK.reshape(4, 2, 80, 640)
+    bk_x = dp_x(BKv)
 
     def assemble(src, dst1, dst2):
         for g in range(8):
@@ -533,7 +564,9 @@
     lax.fori_loop(0, 8, head_group, 0)
 
     dp_done(GCv, gc_c)
-    cl_ref[...] = ((GC[0] + GC[1]) + (GC[2] + GC[3])) + ((GC[4] + GC[5]) + (GC[6] + GC[7]))
+    cl_sum = ((GC[0] + GC[1]) + (GC[2] + GC[3])) + ((GC[4] + GC[5]) + (GC[6] + GC[7]))
+    for k in range(4):
+        cl_ref[:, 1024 * k : 1024 * k + 1024] = cl_sum[2 * k : 2 * k + 2, :]
 
     both = BK[d].astype(F32)
     b1a, b1b = both[0:40, :].astype(BF16), both[40:80, 0:384].astype(BF16)
@@ -565,26 +598,27 @@
         copy.wait_send()
 
 
+def hand_over(*refs):
+    copies = [pltpu.make_async_copy(refs[i], refs[8 + i], refs[16].at[i]) for i in range(8)]
+    for copy in copies:
+        copy.start()
+    for copy in copies:
+        copy.wait()
+
+
 def on_device(
     hidden_states, head_weight, cluster_weight, proj_one, tail_one, proj_two, tail_two,
     targets, token_cluster, tail_rows, tail_counts,
 ):
-    slot = jnp.arange(40, dtype=jnp.int32)[None, :]
-    rows = jnp.where(slot < tail_counts[0][:, None], tail_rows[0], -1).reshape(1, 80)
-    meta = jnp.concatenate(
-        [
-            jnp.pad(jnp.stack([targets, token_cluster]), ((0, 6), (0, 96)), constant_values=-1),
-            jnp.pad(rows, ((0, 7), (0, 48)), constant_values=-1),
-        ],
-        axis=1,
-    )
     vmem = pl.BlockSpec(memory_space=pltpu.VMEM)
+    hbm = pl.BlockSpec(memory_space=pl.ANY)
     shapes = [
-        ((1, 256), F32), ((64, 160), F32), ((160, 512), F32), ((8, 1024), F32),
+        ((1, 160), F32), ((64, 160), F32), ((160, 512), F32), ((2, 4096), F32),
         ((64, 1024), F32), ((320, 128), F32), ((64, 256), F32), ((32, 1664), F32),
     ]
     V = pltpu.VMEM
     scratch = [
+        V((320, 1024), BF16), V((1664, 256), BF16), V((2, 256), jnp.int32),
         V((64, 256), F32), V((4, 4, 4, 80, 128), BF16), V((4096, 256), BF16), V((256, 4096), BF16),
         V((4096, 256), BF16), V((8, 4, 2, 80, 128), BF16), V((512, 256), BF16),
         V((8, 80, 128), BF16), V((4, 4, 4, 8, 128), F32), V((3, 4, 4, 8, 128), F32),
@@ -598,27 +632,35 @@
         V((4, 4, 8, 128), F32), V((4, 8, 128), F32), V((4, 4, 4, 8, 128), F32), V((8, 80, 640), BF16),
         V((320, 128), F32), V((320, 128), F32),
         V((4, 4, 4, 80, 128), BF16), V((3, 4, 4, 80, 128), BF16), V((3, 4, 80, 128), BF16),
-        V((3, 4, 80, 128), BF16), V((4, 80, 128), F32), V((7, 80, 128), BF16),
+        V((3, 4, 80, 128), BF16), V((4, 80, 128), F32), V((6, 80, 128), BF16),
         pltpu.SemaphoreType.DMA((SEMS,)), pltpu.SemaphoreType.DMA((SEMS,)), pltpu.SemaphoreType.DMA,
+        pltpu.SemaphoreType.DMA((2,)),
     ]
     out = pl.pallas_call(
         kernel,
         out_shape=[jax.ShapeDtypeStruct(s, t) for s, t in shapes],
-        in_specs=[vmem, pl.BlockSpec(memory_space=pl.ANY)] + [vmem] * 6,
+        in_specs=[vmem, hbm, vmem, vmem, hbm, vmem, hbm] + [vmem] * 4,
         out_specs=[vmem] * 8,
         scratch_shapes=scratch,
         compiler_params=pltpu.CompilerParams(
             collective_id=0, has_side_effects=True, vmem_limit_bytes=56 * 1024 * 1024
         ),
     )(
-        hidden_states.T, head_weight, cluster_weight, proj_one, tail_one, proj_two, tail_two, meta
+        hidden_states.T, head_weight, cluster_weight, proj_one, tail_one, proj_two, tail_two,
+        targets.reshape(1, 160), token_cluster.reshape(1, 160), tail_rows[0], tail_counts,
     )
-    loss, gh, head, cl, gp1, gt1, gp2, gt2 = out
+    loss, gh, head, cl, gp1, gt1, gp2, gt2 = pl.pallas_call(
+        hand_over,
+        out_shape=[jax.ShapeDtypeStruct(s, t) for s, t in shapes],
+        in_specs=[hbm] * 8,
+        out_specs=[hbm] * 8,
+        scratch_shapes=[pltpu.SemaphoreType.DMA((8,))],
+    )(*out)
     return (
-        loss[0, :160],
+        loss.reshape(160),
         gh.T,
         head,
-        cl.reshape(4, 2, 1024).transpose(1, 0, 2).reshape(2, 4096),
+        cl,
         gp1,
         gt1,
         gp2,

time: 137 us -> 152 us (1.11)
  Pallas kernels: 123 us -> 151 us
  local copies, waits for them, and re-layouts: 10.4 us -> 0 us
  other arithmetic: 2.04 us -> 0 us
    pallas_call x0 -> x1, Pallas kernels: none -> 35.5 us  [on_device(): pl.pallas_call(hand_over, out_shape=[jax.ShapeDtypeStruct(s, t) for s, t...]
    unnamed x13 -> x0, local copies, waits for them, and re-layouts: 8.07 us -> none
    pallas_call x1, Pallas kernels: 123 us -> 116 us  [on_device(): pl.pallas_call(kernel, out_shape=[jax.ShapeDtypeStruct(s, t) for s, t in...]
where the time goes in v2:
time: 152 us
  Pallas kernels  151 us (99%)
    pallas_call x1, Pallas kernels, on_device(): pl.pallas_call(kernel, out_shape=[jax.ShapeDtypeStruct(s, t) for s, t in...  116 us
    pallas_call x1, Pallas kernels, on_device(): pl.pallas_call(hand_over, out_shape=[jax.ShapeDtypeStruct(s, t) for s, t...  35.5 us

profile of v2, /device:TPU:1, one launch (start us, length us, event | category | flops | bytes accessed | tf_op | source)
XLA Modules:
  0.0 151.7 jit_solution(11605697945938237574)
XLA Ops:
  0.6 115.6 %shard_map.170 = (f32[1,160]{1,0:T(1,128)}, f32[64,160]{1,0:T(8,128)}, f32[160,512]{1,0:T(8,128)}, f32[2,4096]{1,0:T(2,128)}, f32[64,1024]{1,0:T(8,128)}, /*inde...) custom-call(bf16[64,160]{1,0:T(8,128)(2,1)} %bitcast.7, bf16[160,4096]{1,0:T(8,128)(2,1)} %hw_ref.1, ...), custom_call_target="tpu_custom_call" | custom-call | tf_op jit(solution)/shard_map/pallas_call | solution.py:639
  116.3 35.5 %shard_map.171 = (f32[1,160]{1,0:T(1,128)}, f32[64,160]{1,0:T(8,128)}, f32[160,512]{1,0:T(8,128)}, f32[2,4096]{1,0:T(2,128)}, f32[64,1024]{1,0:T(8,128)}, /*inde...) custom-call(f32[1,160]{1,0:T(1,128)} %get-tuple-element.24.refs_0_, f32[64,160]{1,0:T(8,128)} %get-tuple-element.25.refs_1_, ...), custom_call_target="tpu_custom_call" | custom-call | tf_op jit(solution)/shard_map/pallas_call | solution.py:652

commit v3 on v2

--- a/solution.py
+++ b/solution.py
@@ -57,11 +57,11 @@
     hid_ref, hw_ref, cw_ref, p1_ref, t1_hbm, p2_ref, t2_hbm, tgt_ref, clu_ref, rows_ref, count_ref,
     loss_ref, gh_ref, head_ref, cl_ref, gp1_ref, gt1_ref, gp2_ref, gt2_ref,
     t1_ref, t2_ref, ids, hp, G, WT, hwx, hwxT, HG, HU,
-    CH, PT, PRY, PRN, PRF, PS1, PS2, PG, Xf, PJ,
+    CH, PT, PRY, PRN, PRF, PS1, PG, Xf, PJ,
     P1f, P2f, P1b, P2b,
-    ST, STF, STN, STY, TS,
+    STF, STN, STY, TTF, TTN, TTY, TS,
     LG, L1s, L2s, INF, GP, GU, GC,
-    BT, BRY, BRN, BRF, BS1, BS2, BG, BK, C1f, C2f,
+    BT, BRY, BRN, BRF, BS1, BG, BK, C1f, C2f,
     GB, GRY, GS1, GRN, GS2, GRF,
     ssem, rsem, lsem, tsem,
 ):
@@ -189,42 +189,29 @@
             for n, o in enumerate(NEAR)
         ]
 
-    def small_far(sums, nslots, ids, sums2, fslots):
+    def small_far(sums, nslots, ids, fslots):
         for n, i in enumerate(ids):
             recv(i, nslots.at[n])
-        sums2[...] = (sums[zlo] + nslots[0]) + (nslots[1] + nslots[2])
-        return [
-            send(sums2.at[lax.rem(zhi + k, 4)], fslots.at[k - 1], far_dev(k)) for k in FAR
-        ]
-
-    def small_sum_y(sums2, fslots, ids, full):
-        for n, i in enumerate(ids):
-            recv(i, fslots.at[n])
-        full[y, zlo, zhi] = (sums2[zhi] + fslots[0]) + (fslots[1] + fslots[2])
-        return [send(full.at[y, zlo, zhi], full.at[y, zlo, zhi], y_dev(k)) for k in FAR]
-
-    def small_spread_far(full, ids):
+        fslots[zhi] = (sums[zlo] + nslots[0]) + (nslots[1] + nslots[2])
+        return [send(fslots.at[zhi], fslots.at[zhi], far_dev(k)) for k in FAR]
+
+    def small_total(fslots, ids, full):
         for k, i in zip(FAR, ids):
-            recv(i, full.at[lax.rem(y + 4 - k, 4), zlo, zhi])
-        return [send(full.at[:, zlo, zhi], full.at[:, zlo, zhi], far_dev(k)) for k in FAR]
-
-    def small_spread_near(full, ids):
+            recv(i, fslots.at[lax.rem(zhi + 4 - k, 4)])
+        full[y, zlo] = (fslots[0] + fslots[1]) + (fslots[2] + fslots[3])
+
+    def back_y_first(full):
+        return [send(full.at[y, zlo], full.at[y, zlo], y_dev(k)) for k in FAR]
+
+    def back_near_second(full, ids):
         for k, i in zip(FAR, ids):
-            recv(i, full.at[:, zlo, lax.rem(zhi + 4 - k, 4)])
+            recv(i, full.at[lax.rem(y + 4 - k, 4), zlo])
         return [send(full.at[:, zlo], full.at[:, zlo], near_dev(o)) for o in NEAR]
 
-    def small_sum_far(sums2, fslots, ids, full):
-        for n, i in enumerate(ids):
-            recv(i, fslots.at[n])
-        full[y, zlo, zhi] = (sums2[zhi] + fslots[0]) + (fslots[1] + fslots[2])
-        return [send(full.at[y, zlo, zhi], full.at[y, zlo, zhi], far_dev(k)) for k in FAR]
-
-    def small_back_near(full, ids):
-        for k, i in zip(FAR, ids):
-            recv(i, full.at[y, zlo, lax.rem(zhi + 4 - k, 4)])
+    def back_near_first(full):
         return [send(full.at[y, zlo], full.at[y, zlo], near_dev(o)) for o in NEAR]
 
-    def small_back_y(full, ids):
+    def back_y_second(full, ids):
         for o, i in zip(NEAR, ids):
             recv(i, full.at[y, lax.rem(zlo + 16 - o, 4)])
         return [send(full.at[y], full.at[y], y_dev(k)) for k in FAR]
@@ -276,24 +263,29 @@
 
     pr_n = small_near(PT, PRY, pr_y, PS1, PRN)
     lax.fori_loop(0, 8, turn, 0)
+    pr_f = small_far(PS1, PRN, pr_n, PRF)
     for k, i in zip(FAR, hid_far):
         recv(i, G.at[y, zlo, lax.rem(zhi + 4 - k, 4)])
     hid_near = [send(G.at[y, zlo], G.at[y, zlo], near_dev(o)) for o in NEAR]
-    pr_f = small_far(PS1, PRN, pr_n, PS2, PRF)
     hid_y = [[send(G.at[y, zlo], G.at[y, zlo], y_dev(k)) for k in FAR]]
-    lax.fori_loop(8, 16, turn, 0)
-    pr_by = small_sum_y(PS2, PRF, pr_f, PG)
-    for o, i in zip(NEAR, hid_near):
-        at = lax.rem(zlo + 16 - o, 4)
-        recv(i, G.at[y, at])
+    lax.fori_loop(8, 20, turn, 0)
+    spread(y, zlo)
+
+    def pass_on(n):
+        at = lax.rem(zlo + 16 - NEAR[n], 4)
+        recv(hid_near[n], G.at[y, at])
         hid_y.append([send(G.at[y, at], G.at[y, at], y_dev(k)) for k in FAR])
-    pr_bf = small_spread_far(PG, pr_by)
-    lax.fori_loop(16, 24, turn, 0)
-    pr_bn = small_spread_near(PG, pr_bf)
+
+    pass_on(0)
+    small_total(PRF, pr_f, PG)
+    pr_by = back_y_first(PG)
+    pass_on(1)
+    pass_on(2)
+    pr_bn = back_near_second(PG, pr_by)
     ch_c = dp_core(CHv, ch_x)
-    lax.fori_loop(24, 32, turn, 0)
-    for zl in range(4):
-        spread(y, zl)
+    lax.fori_loop(20, 32, turn, 0)
+    for n in range(3):
+        spread(y, lax.rem(zlo + 16 - NEAR[n], 4))
     small_done(PG, [(i, slice(None), lax.rem(zlo + 16 - o, 4)) for o, i in zip(NEAR, pr_bn)])
     PJ[d] = Xf[...].astype(BF16)
     PJv = PJ.reshape(4, 2, 80, 640)
@@ -318,10 +310,43 @@
     lane = lanes((80, 128))
     table = jnp.zeros((80, 128), F32)
     for n in range(3):
-        table = jnp.where(lane == 3 + n, jnp.concatenate([stat1[n], stat2[n]], axis=0), table)
+        table = jnp.where(lane == n, jnp.concatenate([stat1[n], stat2[n]], axis=0), table)
     TS[0:80, :] = table
     TS[80:128, :] = jnp.zeros((48, 128), F32)
-    tail_tile = jnp.transpose(TS[...])[0:8, :]
+    TTF[zhi] = jnp.transpose(TS[...])[0:8, :]
+    tail_ids = [send(TTF.at[zhi], TTF.at[zhi], far_dev(k)) for k in FAR]
+
+    def join(slots):
+        parts = [slots[i] for i in range(4)]
+        m = [p[0:1] for p in parts]
+        top = jnp.maximum(jnp.maximum(m[0], m[1]), jnp.maximum(m[2], m[3]))
+        s = [p[1:2] * jnp.exp(mm - top) for p, mm in zip(parts, m)]
+        t = [p[2:3] for p in parts]
+        return top, (s[0] + s[1]) + (s[2] + s[3]), (t[0] + t[1]) + (t[2] + t[3])
+
+    def as_tile(result):
+        row = rows_of((8, result[0].shape[1]))
+        return jnp.where(
+            row == 0, result[0], jnp.where(row == 1, result[1], jnp.where(row == 2, result[2], 0.0))
+        )
+
+    def join_far(far, near, ids):
+        for k, i in zip(FAR, ids):
+            recv(i, far.at[lax.rem(zhi + 4 - k, 4)])
+        near[zlo] = as_tile(join(far))
+        return [send(near.at[zlo], near.at[zlo], near_dev(o)) for o in NEAR]
+
+    def join_near(near, last, ids):
+        for o, i in zip(NEAR, ids):
+            recv(i, near.at[lax.rem(zlo + 16 - o, 4)])
+        last[y] = as_tile(join(near))
+        return [send(last.at[y], last.at[y], y_dev(k)) for k in FAR]
+
+    def join_last(last, ids):
+        for k, i in zip(FAR, ids):
+            recv(i, last.at[lax.rem(y + 4 - k, 4)])
+        return join(last)
+
 
     for n, ids_y in enumerate(hid_y):
         at = zlo if n == 0 else lax.rem(zlo + 16 - NEAR[n - 1], 4)
@@ -343,48 +368,17 @@
     high = jnp.max(words, axis=0, keepdims=True)
     total = jnp.sum(jnp.exp(words - high), axis=0, keepdims=True)
     picked = jnp.sum(jnp.where(head_hit, words, 0.0), axis=0, keepdims=True)
-    row8 = rows_of((8, 256))
-    wide_tail = jnp.concatenate([tail_tile, jnp.zeros((8, 128), F32)], axis=1)
-    tile = jnp.where(
-        row8 == 0, high, jnp.where(row8 == 1, total, jnp.where(row8 == 2, picked, wide_tail))
-    )
-
-    def join(slots):
-        parts = [slots[i] for i in range(4)]
-        result = []
-        for base in (0, 3):
-            m = [p[base : base + 1] for p in parts]
-            top = jnp.maximum(jnp.maximum(m[0], m[1]), jnp.maximum(m[2], m[3]))
-            s = [p[base + 1 : base + 2] * jnp.exp(mm - top) for p, mm in zip(parts, m)]
-            t = [p[base + 2 : base + 3] for p in parts]
-            result += [top, (s[0] + s[1]) + (s[2] + s[3]), (t[0] + t[1]) + (t[2] + t[3])]
-        return result
-
-    def as_tile(result):
-        out = jnp.zeros((8, 256), F32)
-        for n in range(6):
-            out = jnp.where(row8 == n, result[n], out)
-        return out
-
-    STF[zhi] = tile
-    near_ids = [send(STF.at[zhi], STF.at[zhi], far_dev(k)) for k in FAR]
+    STF[zhi] = as_tile((high, total, picked))
+    head_ids = [send(STF.at[zhi], STF.at[zhi], far_dev(k)) for k in FAR]
+    tail_ids = join_far(TTF, TTN, tail_ids)
     pj_c = dp_core(PJv, pj_x)
-    for k, i in zip(FAR, near_ids):
-        recv(i, STF.at[lax.rem(zhi + 4 - k, 4)])
-    STN[zlo] = as_tile(join(STF))
-    near_ids = [send(STN.at[zlo], STN.at[zlo], near_dev(o)) for o in NEAR]
-    for o, i in zip(NEAR, near_ids):
-        recv(i, STN.at[lax.rem(zlo + 16 - o, 4)])
-    STY[y] = as_tile(join(STN))
-    near_ids = [send(STY.at[y], STY.at[y], y_dev(k)) for k in FAR]
-    for k, i in zip(FAR, near_ids):
-        recv(i, STY.at[lax.rem(y + 4 - k, 4)])
-    stats = join(STY)
-
-    tail_lse = stats[3] + jnp.log(stats[4])
+    tail_ids = join_near(TTN, TTY, tail_ids)
+    tail_stats = join_last(TTY, tail_ids)
+
+    tail_lse = tail_stats[0] + jnp.log(tail_stats[1])
     TS[...] = jnp.zeros_like(TS)
-    TS[0:1, :] = tail_lse[:, 0:128]
-    TS[1:2, :] = (tail_lse - stats[5])[:, 0:128]
+    TS[0:1, :] = tail_lse
+    TS[1:2, :] = tail_lse - tail_stats[2]
     columns = jnp.transpose(TS[...])[0:80, :]
     lse_col = jnp.where(live, columns[:, 0:1], 1e30)
     loss_col = columns[:, 1:2]
@@ -394,15 +388,18 @@
         return (SCALE * (jnp.exp(values - lse) - hit)).astype(BF16)
 
     own1 = tail_gradient(L1s[...], lse_col[0:40], goal[0:40] - v * 320)
-    own2 = tail_gradient(L2s[...], lse_col[40:80], jnp.where(live, goal, -(1 << 20))[40:80] - v * 1664)
-    back1 = dot(own1, t1_ref[...])
-    back2 = dot(own2, t2_ref[...])
-    to_tiles(BT, back1, back2)
+    own2 = tail_gradient(L2s[...], lse_col[40:80], goal[40:80] - v * 1664)
+    to_tiles(BT, dot(own1, t1_ref[...]), dot(own2, t2_ref[...]))
     bk_y = small_y(BT, BRY)
 
     INF[d] = jnp.where(lane == 0, lse_col, jnp.where(lane == 1, goal.astype(F32), 0.0))
     INFv = INF.reshape(4, 2, 80, 128)
     inf_x = dp_x(INFv)
+    head_ids = join_far(STF, STN, head_ids)
+    bk_n = small_near(BT, BRY, bk_y, BS1, BRN)
+    head_ids = join_near(STN, STY, head_ids)
+    bk_f = small_far(BS1, BRN, bk_n, BRF)
+    stats = join_last(STY, head_ids)
 
     entry0, entry1 = LG[160:161, :], LG[161:162, :]
     top = jnp.maximum(stats[0], jnp.maximum(entry0, entry1))
@@ -446,10 +443,8 @@
         )
 
     part(NEAR[0])
-    bk_n = small_near(BT, BRY, bk_y, BS1, BRN)
     part(NEAR[1])
     part(NEAR[2])
-    bk_f = small_far(BS1, BRN, bk_n, BS2, BRF)
     part(0)
     entries = jnp.where(rows_of((8, 256)) % 2 == 0, ge0, ge1).astype(BF16)
     full = dot(entries, WT[...], NT)
@@ -460,7 +455,8 @@
     GC[d] = packed_cl
     GCv = GC.reshape(4, 2, 8, 1024)
     gc_x = dp_x(GCv)
-    bk_bf = small_sum_far(BS2, BRF, bk_f, BG)
+    small_total(BRF, bk_f, BG)
+    bk_bn = back_near_first(BG)
     inf_c = dp_core(INFv, inf_x)
     gp_c = dp_core(GPv, gp_x)
 
@@ -477,9 +473,8 @@
         gh_n.append(send(GS1.at[n], GRN.at[n], near_dev(NEAR[n])))
 
     chunk_near(0)
-    bk_bn = small_back_near(BG, bk_bf)
+    bk_by = back_y_second(BG, bk_bn)
     chunk_near(1)
-    bk_by = small_back_y(BG, bk_bn)
     chunk_near(2)
     gc_c = dp_core(GCv, gc_x)
     for k, i in zip(FAR, gh_y[3]):
@@ -599,11 +594,8 @@
 
 
 def hand_over(*refs):
-    copies = [pltpu.make_async_copy(refs[i], refs[8 + i], refs[16].at[i]) for i in range(8)]
-    for copy in copies:
-        copy.start()
-    for copy in copies:
-        copy.wait()
+    for i in range(8):
+        refs[8 + i][...] = refs[i][...]
 
 
 def on_device(
@@ -622,14 +614,15 @@
         V((64, 256), F32), V((4, 4, 4, 80, 128), BF16), V((4096, 256), BF16), V((256, 4096), BF16),
         V((4096, 256), BF16), V((8, 4, 2, 80, 128), BF16), V((512, 256), BF16),
         V((8, 80, 128), BF16), V((4, 4, 4, 8, 128), F32), V((3, 4, 4, 8, 128), F32),
-        V((3, 4, 8, 128), F32), V((3, 8, 128), F32), V((4, 4, 8, 128), F32), V((4, 8, 128), F32),
+        V((3, 4, 8, 128), F32), V((4, 4, 8, 128), F32), V((4, 4, 8, 128), F32),
         V((4, 4, 4, 8, 128), F32), V((80, 640), F32), V((8, 80, 640), BF16),
         V((320, 1024), F32), V((320, 256), F32), V((320, 1024), BF16), V((320, 256), BF16),
-        V((8, 256), F32), V((4, 8, 256), F32), V((4, 8, 256), F32), V((4, 8, 256), F32), V((128, 128), F32),
+        V((4, 8, 256), F32), V((4, 8, 256), F32), V((4, 8, 256), F32),
+        V((4, 8, 128), F32), V((4, 8, 128), F32), V((4, 8, 128), F32), V((128, 128), F32),
         V((256, 256), F32), V((40, 320), F32), V((40, 1664), F32), V((8, 80, 128), F32),
         V((8, 208, 128), BF16), V((160, 256), BF16), V((8, 8, 1024), F32),
-        V((4, 4, 4, 8, 128), F32), V((3, 4, 4, 8, 128), F32), V((3, 4, 8, 128), F32), V((3, 8, 128), F32),
-        V((4, 4, 8, 128), F32), V((4, 8, 128), F32), V((4, 4, 4, 8, 128), F32), V((8, 80, 640), BF16),
+        V((4, 4, 4, 8, 128), F32), V((3, 4, 4, 8, 128), F32), V((3, 4, 8, 128), F32), V((4, 4, 8, 128), F32),
+        V((4, 4, 8, 128), F32), V((4, 4, 4, 8, 128), F32), V((8, 80, 640), BF16),
         V((320, 128), F32), V((320, 128), F32),
         V((4, 4, 4, 80, 128), BF16), V((3, 4, 4, 80, 128), BF16), V((3, 4, 80, 128), BF16),
         V((3, 4, 80, 128), BF16), V((4, 80, 128), F32), V((6, 80, 128), BF16),
@@ -652,9 +645,8 @@
     loss, gh, head, cl, gp1, gt1, gp2, gt2 = pl.pallas_call(
         hand_over,
         out_shape=[jax.ShapeDtypeStruct(s, t) for s, t in shapes],
-        in_specs=[hbm] * 8,
-        out_specs=[hbm] * 8,
-        scratch_shapes=[pltpu.SemaphoreType.DMA((8,))],
+        in_specs=[vmem] * 8,
+        out_specs=[vmem] * 8,
     )(*out)
     return (
         loss.reshape(160),

time: 152 us -> 104 us (0.68)
  Pallas kernels: 151 us -> 103 us
    pallas_call x1, Pallas kernels: 35.5 us -> 2.27 us  [on_device(): pl.pallas_call(hand_over, out_shape=[jax.ShapeDtypeStruct(s, t) for s, t...]
    pallas_call x1, Pallas kernels: 116 us -> 100 us  [on_device(): pl.pallas_call(kernel, out_shape=[jax.ShapeDtypeStruct(s, t) for s, t in...]
where the time goes in v3:
time: 104 us; the launch traced here: 103 us
  Pallas kernels  103 us (99%)
    pallas_call x1, Pallas kernels, on_device(): pl.pallas_call(kernel, out_shape=[jax.ShapeDtypeStruct(s, t) for s, t in...  100 us
    pallas_call x1, Pallas kernels, on_device(): pl.pallas_call(hand_over, out_shape=[jax.ShapeDtypeStruct(s, t) for s, t...  2.27 us

profile of v3, /device:TPU:1, one launch (start us, length us, event | category | flops | bytes accessed | tf_op | source)
XLA Modules:
  0.0 103.2 jit_solution(7935098860605860774)
XLA Ops:
  0.6 100.2 %shard_map.170 = (f32[1,160]{1,0:T(1,128)}, f32[64,160]{1,0:T(8,128)}, f32[160,512]{1,0:T(8,128)}, f32[2,4096]{1,0:T(2,128)}, f32[64,1024]{1,0:T(8,128)}, /*inde...) custom-call(bf16[64,160]{1,0:T(8,128)(2,1)} %bitcast.7, bf16[160,4096]{1,0:T(8,128)(2,1)} %hw_ref.1, ...), custom_call_target="tpu_custom_call" | custom-call | tf_op jit(solution)/shard_map/pallas_call | solution.py:632
  100.9 2.3 %shard_map.171 = (f32[1,160]{1,0:T(1,128)}, f32[64,160]{1,0:T(8,128)}, f32[160,512]{1,0:T(8,128)}, f32[2,4096]{1,0:T(2,128)}, f32[64,1024]{1,0:T(8,128)}, /*inde...) custom-call(f32[1,160]{1,0:T(1,128)} %get-tuple-element.24.refs_0_, f32[64,160]{1,0:T(8,128)} %get-tuple-element.25.refs_1_, ...), custom_call_target="tpu_custom_call" | custom-call | tf_op jit(solution)/shard_map/pallas_call | solution.py:645

commit v4 on v3

--- a/solution.py
+++ b/solution.py
@@ -11,8 +11,8 @@
 SCALE = 64.0
 FAR = (1, 2, 3)
 NEAR = (1, 15, 2)
-NEAR_FROM = (15, 1, 14)
-SEMS = 128
+OFFS = (8, 7, 9, 6, 10, 5, 11, 4, 12, 3, 13, 14, 2, 15, 1, 0)
+SEMS = 144
 NT = (((1,), (1,)), ((), ()))
 TN = (((0,), (0,)), ((), ()))
 NN = (((1,), (0,)), ((), ()))
@@ -54,7 +54,9 @@
 
 
 def kernel(
-    hid_ref, hw_ref, cw_ref, p1_ref, t1_hbm, p2_ref, t2_hbm, tgt_ref, clu_ref, rows_ref, count_ref,
+    hid_hbm, hw_ref, cw_ref, p1_hbm, t1_hbm, p2_hbm, t2_hbm, tgt_hbm, clu_hbm, rows_hbm, count_hbm,
+    loss_out, gh_out, head_out, cl_out, gp1_out, gt1_out, gp2_out, gt2_out,
+    hid_ref, p1_ref, p2_ref, tgt_ref, clu_ref, rows_ref, count_ref,
     loss_ref, gh_ref, head_ref, cl_ref, gp1_ref, gt1_ref, gp2_ref, gt2_ref,
     t1_ref, t2_ref, ids, hp, G, WT, hwx, hwxT, HG, HU,
     CH, PT, PRY, PRN, PRF, PS1, PG, Xf, PJ,
@@ -62,8 +64,8 @@
     STF, STN, STY, TTF, TTN, TTY, TS,
     LG, L1s, L2s, INF, GP, GU, GC,
     BT, BRY, BRN, BRF, BS1, BG, BK, C1f, C2f,
-    GB, GRY, GS1, GRN, GS2, GRF,
-    ssem, rsem, lsem, tsem,
+    GB, GRY, GZS, GRZ, GS2,
+    ssem, rsem, lsem, tsem, isem, osem,
 ):
     d = lax.axis_index("dp")
     v = lax.axis_index("vocab")
@@ -108,25 +110,44 @@
             device_id=core_dev, device_id_type=MESH,
         ).wait_recv()
 
-    hw_copy = pltpu.make_async_copy(hw_ref, hwx.at[0:160], lsem)
-    t1_copy = pltpu.make_async_copy(t1_hbm, t1_ref, tsem.at[0])
-    t2_copy = pltpu.make_async_copy(t2_hbm, t2_ref, tsem.at[1])
-    hw_copy.start()
-    t1_copy.start()
-    t2_copy.start()
-
     barrier = pltpu.get_barrier_semaphore()
     greeted = 0
     for k in FAR:
-        pl.semaphore_signal(barrier, inc=1, device_id=far_dev(k), device_id_type=MESH)
         pl.semaphore_signal(barrier, inc=1, device_id=y_dev(k), device_id_type=MESH)
-        greeted += 2
-    for o in NEAR_FROM:
+        greeted += 1
+    for o in (8, 7, 9, 6, 10, 5, 11, 4, 12, 3, 13, 2, 14, 1, 15):
         pl.semaphore_signal(barrier, inc=1, device_id=near_dev(o), device_id_type=MESH)
         greeted += 1
     for k in range(1, 8):
         pl.semaphore_signal(barrier, inc=1, device_id=dp_dev(k), device_id_type=MESH)
         greeted += 1
+
+    loads = [
+        pltpu.make_async_copy(src, dst, isem.at[n])
+        for n, (src, dst) in enumerate(
+            (
+                (hid_hbm, hid_ref), (rows_hbm, rows_ref), (count_hbm, count_ref), (tgt_hbm, tgt_ref),
+                (clu_hbm, clu_ref), (p1_hbm, p1_ref), (p2_hbm, p2_ref),
+            )
+        )
+    ]
+    hw_copy = pltpu.make_async_copy(hw_ref, hwx.at[0:160], lsem)
+    t1_copy = pltpu.make_async_copy(t1_hbm, t1_ref, tsem.at[0])
+    t2_copy = pltpu.make_async_copy(t2_hbm, t2_ref, tsem.at[1])
+    for copy in loads:
+        copy.start()
+    hw_copy.start()
+    t1_copy.start()
+    t2_copy.start()
+    stores = []
+
+    def store(src, dst):
+        copy = pltpu.make_async_copy(src, dst, osem.at[len(stores)])
+        copy.start()
+        stores.append(copy)
+
+    for copy in loads:
+        copy.wait()
 
     hp[...] = jnp.zeros_like(hp)
     hp[:, 0:160] = hid_ref[...].astype(F32)
@@ -373,6 +394,7 @@
     tail_ids = join_far(TTF, TTN, tail_ids)
     pj_c = dp_core(PJv, pj_x)
     tail_ids = join_near(TTN, TTY, tail_ids)
+    head_ids = join_far(STF, STN, head_ids)
     tail_stats = join_last(TTY, tail_ids)
 
     tail_lse = tail_stats[0] + jnp.log(tail_stats[1])
@@ -392,13 +414,11 @@
     to_tiles(BT, dot(own1, t1_ref[...]), dot(own2, t2_ref[...]))
     bk_y = small_y(BT, BRY)
 
+    head_ids = join_near(STN, STY, head_ids)
     INF[d] = jnp.where(lane == 0, lse_col, jnp.where(lane == 1, goal.astype(F32), 0.0))
     INFv = INF.reshape(4, 2, 80, 128)
     inf_x = dp_x(INFv)
-    head_ids = join_far(STF, STN, head_ids)
     bk_n = small_near(BT, BRY, bk_y, BS1, BRN)
-    head_ids = join_near(STN, STY, head_ids)
-    bk_f = small_far(BS1, BRN, bk_n, BRF)
     stats = join_last(STY, head_ids)
 
     entry0, entry1 = LG[160:161, :], LG[161:162, :]
@@ -409,6 +429,7 @@
     chosen_logit = stats[2] + (is1 * entry0 + is2 * entry1)
     tail_loss = jnp.sum(jnp.where(slot_hit, loss_col, 0.0), axis=0, keepdims=True)
     loss_ref[...] = ((lse - chosen_logit) + tail_loss)[:, 0:160]
+    store(loss_ref, loss_out)
 
     inside = lanes((160, 256)) < 160
     grad = jnp.where(inside, SCALE * (jnp.exp(LG[0:160, :] - lse) - head_hit.astype(F32)), 0.0)
@@ -428,24 +449,25 @@
 
     gh_y = []
 
-    def part(o):
-        at = lax.rem(zlo + o, 4)
-        for zh in range(4):
-            rows = pl.ds(pl.multiple_of((zh * 4 + at) * 256, 256), 256)
-            product = dot(hwxT[rows, :], grad_ext)
+    def part(n):
+        for j in range(4 * n, 4 * n + 4):
+            zz = lax.rem(z + OFFS[j], 16)
+            product = dot(hwxT[pl.ds(pl.multiple_of(zz * 256, 256), 256), :], grad_ext)
             for yy in range(4):
-                block = GB.at[yy, at, zh]
+                block = GB.at[yy, j]
                 piece = product[64 * yy : 64 * yy + 64]
                 block[0:64, :] = piece[:, 0:128].astype(BF16)
                 block[64:80, :] = pack_rest(piece[:, 128:256], 16).astype(BF16)
+        at = pl.ds(4 * n, 4)
         gh_y.append(
             [send(GB.at[lax.rem(y + k, 4), at], GRY.at[k - 1, at], y_dev(k)) for k in FAR]
         )
 
-    part(NEAR[0])
-    part(NEAR[1])
-    part(NEAR[2])
     part(0)
+    part(1)
+    bk_f = small_far(BS1, BRN, bk_n, BRF)
+    part(2)
+    part(3)
     entries = jnp.where(rows_of((8, 256)) % 2 == 0, ge0, ge1).astype(BF16)
     full = dot(entries, WT[...], NT)
     pair = lax.div(rows_of((8, 1024)), 2)
@@ -455,41 +477,33 @@
     GC[d] = packed_cl
     GCv = GC.reshape(4, 2, 8, 1024)
     gc_x = dp_x(GCv)
+    inf_c = dp_core(INFv, inf_x)
+    gp_c = dp_core(GPv, gp_x)
+
+    gh_z = []
+
+    def chunk_z(n):
+        at = pl.ds(4 * n, 4)
+        for k, i in zip(FAR, gh_y[n]):
+            recv(i, GRY.at[k - 1, at])
+        for j in range(4 * n, 4 * n + 4):
+            total = (GB[y, j].astype(F32) + GRY[0, j].astype(F32)) + (
+                GRY[1, j].astype(F32) + GRY[2, j].astype(F32)
+            )
+            if OFFS[j]:
+                GZS[j] = total.astype(BF16)
+                gh_z.append(send(GZS.at[j], GRZ.at[j], near_dev(OFFS[j])))
+            else:
+                GS2[...] = total
+
+    chunk_z(0)
     small_total(BRF, bk_f, BG)
     bk_bn = back_near_first(BG)
-    inf_c = dp_core(INFv, inf_x)
-    gp_c = dp_core(GPv, gp_x)
-
-    gh_n = []
-
-    def chunk_near(n):
-        at = lax.rem(zlo + NEAR[n], 4)
-        for k, i in zip(FAR, gh_y[n]):
-            recv(i, GRY.at[k - 1, at])
-        GS1[n] = (
-            (GB[y, at].astype(F32) + GRY[0, at].astype(F32))
-            + (GRY[1, at].astype(F32) + GRY[2, at].astype(F32))
-        ).astype(BF16)
-        gh_n.append(send(GS1.at[n], GRN.at[n], near_dev(NEAR[n])))
-
-    chunk_near(0)
+    chunk_z(1)
     bk_by = back_y_second(BG, bk_bn)
-    chunk_near(1)
-    chunk_near(2)
+    chunk_z(2)
     gc_c = dp_core(GCv, gc_x)
-    for k, i in zip(FAR, gh_y[3]):
-        recv(i, GRY.at[k - 1, zlo])
-    mine_sum = (GB[y, zlo].astype(F32) + GRY[0, zlo].astype(F32)) + (
-        GRY[1, zlo].astype(F32) + GRY[2, zlo].astype(F32)
-    )
-    for n, i in enumerate(gh_n):
-        recv(i, GRN.at[n])
-    GS2[...] = mine_sum + (
-        GRN[0].astype(F32) + (GRN[1].astype(F32) + GRN[2].astype(F32))
-    )
-    for k in FAR:
-        GRF[2 + k] = GS2[lax.rem(zhi + k, 4)].astype(BF16)
-    gh_f = [send(GRF.at[2 + k], GRF.at[k - 1], far_dev(k)) for k in FAR]
+    chunk_z(3)
     small_done(BG, [(i, lax.rem(y + 4 - k, 4), None) for k, i in zip(FAR, bk_by)])
     BK[d] = Xf[...].astype(BF16)
     BKv = BK.reshape(4, 2, 80, 640)
@@ -516,6 +530,7 @@
     base1 = jnp.where(goal1 < 0, -(1 << 20), goal1 - v * 320)
     grad1 = tail_gradient(all1, lse1, base1)
     gt1_ref[...] = dot(grad1, P1b[:, pl.ds(pl.multiple_of(d * 128, 128), 128)], TN)
+    store(gt1_ref, gt1_out)
 
     lse2, goal2 = gather_column(40, 0), gather_column(40, 1).astype(jnp.int32)
     base2 = jnp.where(goal2 < 0, -(1 << 20), goal2 - v * 1664)
@@ -533,6 +548,7 @@
         return 0
 
     lax.fori_loop(0, 13, tail_two, 0)
+    store(gt2_ref, gt2_out)
     bk_c = dp_core(BKv, bk_x)
 
     HG[d] = G[:, pl.ds(lax.rem(2 * d, 4), 2), lax.div(d, 2)]
@@ -557,11 +573,13 @@
         return 0
 
     lax.fori_loop(0, 8, head_group, 0)
+    store(head_ref, head_out)
 
     dp_done(GCv, gc_c)
     cl_sum = ((GC[0] + GC[1]) + (GC[2] + GC[3])) + ((GC[4] + GC[5]) + (GC[6] + GC[7]))
     for k in range(4):
         cl_ref[:, 1024 * k : 1024 * k + 1024] = cl_sum[2 * k : 2 * k + 2, :]
+    store(cl_ref, cl_out)
 
     both = BK[d].astype(F32)
     b1a, b1b = both[0:40, :].astype(BF16), both[40:80, 0:384].astype(BF16)
@@ -570,14 +588,16 @@
     hot2 = jnp.where(slot_hit[40:80], 1.0, 0.0)
     back_one = dot(p1_ref[:, 0:640], b1a, NT) + dot(p1_ref[:, 640:1024], b1b, NT)
     add = dot_exact(back_one, hot1) + dot_exact(dot(p2_ref[...], b2, NT), hot2)
-    for n, i in enumerate(gh_f):
-        recv(i, GRF.at[n])
-    block = GS2[zhi] + (GRF[0].astype(F32) + (GRF[1].astype(F32) + GRF[2].astype(F32)))
+    block = GS2[...]
+    for j, i in enumerate(gh_z):
+        recv(i, GRZ.at[j])
+        block = block + GRZ[j].astype(F32)
     hp[:, 0:128] = block[0:64, :]
     for q in range(4):
         part_q = block[64:80, :]
         hp[16 * q : 16 * q + 16, 128:256] = part_q if q == 0 else pltpu.roll(part_q, 128 - 32 * q, 1)
     gh_ref[...] = (hp[...] + add)[:, 0:160]
+    store(gh_ref, gh_out)
 
     dp_done(CHv, ch_c)
     dp_done(BKv, bk_c)
@@ -587,7 +607,11 @@
         C1f[40 * g : 40 * g + 40, :] = rows_g[0:40, :]
         C2f[40 * g : 40 * g + 40, :] = rows_g[40:80, :]
     gp1_ref[...] = dot(C1f[...].astype(BF16), P1f[...].astype(BF16), TN)[0:64, :]
+    store(gp1_ref, gp1_out)
     gp2_ref[...] = dot(C2f[...].astype(BF16), P2f[...].astype(BF16), TN)[0:64, :]
+    store(gp2_ref, gp2_out)
+    for copy in stores:
+        copy.wait()
 
     for copy in sent:
         copy.wait_send()
@@ -610,6 +634,9 @@
     ]
     V = pltpu.VMEM
     scratch = [
+        V((64, 160), BF16), V((64, 1024), BF16), V((64, 256), BF16), V((1, 160), jnp.int32),
+        V((1, 160), jnp.int32), V((2, 40), jnp.int32), V((1, 2), jnp.int32),
+    ] + [V(s, t) for s, t in shapes] + [
         V((320, 1024), BF16), V((1664, 256), BF16), V((2, 256), jnp.int32),
         V((64, 256), F32), V((4, 4, 4, 80, 128), BF16), V((4096, 256), BF16), V((256, 4096), BF16),
         V((4096, 256), BF16), V((8, 4, 2, 80, 128), BF16), V((512, 256), BF16),
@@ -624,16 +651,16 @@
         V((4, 4, 4, 8, 128), F32), V((3, 4, 4, 8, 128), F32), V((3, 4, 8, 128), F32), V((4, 4, 8, 128), F32),
         V((4, 4, 8, 128), F32), V((4, 4, 4, 8, 128), F32), V((8, 80, 640), BF16),
         V((320, 128), F32), V((320, 128), F32),
-        V((4, 4, 4, 80, 128), BF16), V((3, 4, 4, 80, 128), BF16), V((3, 4, 80, 128), BF16),
-        V((3, 4, 80, 128), BF16), V((4, 80, 128), F32), V((6, 80, 128), BF16),
+        V((4, 16, 80, 128), BF16), V((3, 16, 80, 128), BF16), V((16, 80, 128), BF16),
+        V((16, 80, 128), BF16), V((80, 128), F32),
         pltpu.SemaphoreType.DMA((SEMS,)), pltpu.SemaphoreType.DMA((SEMS,)), pltpu.SemaphoreType.DMA,
-        pltpu.SemaphoreType.DMA((2,)),
+        pltpu.SemaphoreType.DMA((2,)), pltpu.SemaphoreType.DMA((7,)), pltpu.SemaphoreType.DMA((8,)),
     ]
     out = pl.pallas_call(
         kernel,
         out_shape=[jax.ShapeDtypeStruct(s, t) for s, t in shapes],
-        in_specs=[vmem, hbm, vmem, vmem, hbm, vmem, hbm] + [vmem] * 4,
-        out_specs=[vmem] * 8,
+        in_specs=[hbm, hbm, vmem] + [hbm] * 8,
+        out_specs=[hbm] * 8,
         scratch_shapes=scratch,
         compiler_params=pltpu.CompilerParams(
             collective_id=0, has_side_effects=True, vmem_limit_bytes=56 * 1024 * 1024

time: 104 us -> 105 us (level)
  no operation moved by 1% of the time
where the time goes in v4:
time: 105 us; the launch traced here: 104 us
  Pallas kernels  103 us (98%)
    pallas_call x1, Pallas kernels, on_device(): pl.pallas_call(kernel, out_shape=[jax.ShapeDtypeStruct(s, t) for s, t in...  101 us
    pallas_call x1, Pallas kernels, on_device(): pl.pallas_call(hand_over, out_shape=[jax.ShapeDtypeStruct(s, t) for s, t...  2.27 us

profile of v4, /device:TPU:1, one launch (start us, length us, event | category | flops | bytes accessed | tf_op | source)
XLA Modules:
  0.0 103.9 jit_solution(9410216901322559866)
XLA Ops:
  0.6 101.0 %shard_map.170 = (f32[1,160]{1,0:T(1,128)}, f32[64,160]{1,0:T(8,128)}, f32[160,512]{1,0:T(8,128)}, f32[2,4096]{1,0:T(2,128)}, f32[64,1024]{1,0:T(8,128)}, /*inde...) custom-call(bf16[64,160]{1,0:T(8,128)(2,1)} %bitcast.7, bf16[160,4096]{1,0:T(8,128)(2,1)} %hw_ref.1, ...), custom_call_target="tpu_custom_call" | custom-call | tf_op jit(solution)/shard_map/pallas_call | solution.py:659
  101.6 2.3 %shard_map.171 = (f32[1,160]{1,0:T(1,128)}, f32[64,160]{1,0:T(8,128)}, f32[160,512]{1,0:T(8,128)}, f32[2,4096]{1,0:T(2,128)}, f32[64,1024]{1,0:T(8,128)}, /*inde...) custom-call(f32[1,160]{1,0:T(1,128)} %get-tuple-element.24.refs_0_, f32[64,160]{1,0:T(8,128)} %get-tuple-element.25.refs_1_, ...), custom_call_target="tpu_custom_call" | custom-call | tf_op jit(solution)/shard_map/pallas_call | solution.py:672

commit v5 on v4

--- a/solution.py
+++ b/solution.py
@@ -497,18 +497,6 @@
                 GS2[...] = total
 
     chunk_z(0)
-    small_total(BRF, bk_f, BG)
-    bk_bn = back_near_first(BG)
-    chunk_z(1)
-    bk_by = back_y_second(BG, bk_bn)
-    chunk_z(2)
-    gc_c = dp_core(GCv, gc_x)
-    chunk_z(3)
-    small_done(BG, [(i, lax.rem(y + 4 - k, 4), None) for k, i in zip(FAR, bk_by)])
-    BK[d] = Xf[...].astype(BF16)
-    BKv = BK.reshape(4, 2, 80, 640)
-    bk_x = dp_x(BKv)
-
     def assemble(src, dst1, dst2):
         for g in range(8):
             both = src[g].astype(F32)
@@ -547,10 +535,16 @@
         gt2_ref[:, pl.ds(at, 128)] = dot(mine2, grads)
         return 0
 
-    lax.fori_loop(0, 13, tail_two, 0)
+    chunk_z(1)
+    small_total(BRF, bk_f, BG)
+    bk_bn = back_near_first(BG)
+    lax.fori_loop(0, 7, tail_two, 0)
+    chunk_z(2)
+    bk_by = back_y_second(BG, bk_bn)
+    gc_c = dp_core(GCv, gc_x)
+    lax.fori_loop(7, 13, tail_two, 0)
     store(gt2_ref, gt2_out)
-    bk_c = dp_core(BKv, bk_x)
-
+    chunk_z(3)
     HG[d] = G[:, pl.ds(lax.rem(2 * d, 4), 2), lax.div(d, 2)]
     dp_done(GPv, gp_c)
     for k, i in zip(range(1, 8), slices):
@@ -574,6 +568,11 @@
 
     lax.fori_loop(0, 8, head_group, 0)
     store(head_ref, head_out)
+
+    small_done(BG, [(i, lax.rem(y + 4 - k, 4), None) for k, i in zip(FAR, bk_by)])
+    BK[d] = Xf[...].astype(BF16)
+    BKv = BK.reshape(4, 2, 80, 640)
+    bk_x = dp_x(BKv)
 
     dp_done(GCv, gc_c)
     cl_sum = ((GC[0] + GC[1]) + (GC[2] + GC[3])) + ((GC[4] + GC[5]) + (GC[6] + GC[7]))
@@ -598,6 +597,8 @@
         hp[16 * q : 16 * q + 16, 128:256] = part_q if q == 0 else pltpu.roll(part_q, 128 - 32 * q, 1)
     gh_ref[...] = (hp[...] + add)[:, 0:160]
     store(gh_ref, gh_out)
+
+    bk_c = dp_core(BKv, bk_x)
 
     dp_done(CHv, ch_c)
     dp_done(BKv, bk_c)

time: 105 us -> 107 us (1.019)
  Pallas kernels: 103 us -> 106 us
    pallas_call x1, Pallas kernels: 101 us -> 104 us  [on_device(): pl.pallas_call(kernel, out_shape=[jax.ShapeDtypeStruct(s, t) for s, t in...]
where the time goes in v5:
time: 107 us
  Pallas kernels  106 us (99%)
    pallas_call x1, Pallas kernels, on_device(): pl.pallas_call(kernel, out_shape=[jax.ShapeDtypeStruct(s, t) for s, t in...  104 us
    pallas_call x1, Pallas kernels, on_device(): pl.pallas_call(hand_over, out_shape=[jax.ShapeDtypeStruct(s, t) for s, t...  2.27 us

profile of v5, /device:TPU:1, one launch (start us, length us, event | category | flops | bytes accessed | tf_op | source)
XLA Modules:
  0.0 106.7 jit_solution(15730521868381593006)
XLA Ops:
  0.6 103.8 %shard_map.170 = (f32[1,160]{1,0:T(1,128)}, f32[64,160]{1,0:T(8,128)}, f32[160,512]{1,0:T(8,128)}, f32[2,4096]{1,0:T(2,128)}, f32[64,1024]{1,0:T(8,128)}, /*inde...) custom-call(bf16[64,160]{1,0:T(8,128)(2,1)} %bitcast.7, bf16[160,4096]{1,0:T(8,128)(2,1)} %hw_ref.1, ...), custom_call_target="tpu_custom_call" | custom-call | tf_op jit(solution)/shard_map/pallas_call | solution.py:660
  104.4 2.3 %shard_map.171 = (f32[1,160]{1,0:T(1,128)}, f32[64,160]{1,0:T(8,128)}, f32[160,512]{1,0:T(8,128)}, f32[2,4096]{1,0:T(2,128)}, f32[64,1024]{1,0:T(8,128)}, /*inde...) custom-call(f32[1,160]{1,0:T(1,128)} %get-tuple-element.24.refs_0_, f32[64,160]{1,0:T(8,128)} %get-tuple-element.25.refs_1_, ...), custom_call_target="tpu_custom_call" | custom-call | tf_op jit(solution)/shard_map/pallas_call | solution.py:673

commit v6 on v5

--- a/solution.py
+++ b/solution.py
@@ -11,7 +11,7 @@
 SCALE = 64.0
 FAR = (1, 2, 3)
 NEAR = (1, 15, 2)
-OFFS = (8, 7, 9, 6, 10, 5, 11, 4, 12, 3, 13, 14, 2, 15, 1, 0)
+NEAR_FROM = (15, 1, 14)
 SEMS = 144
 NT = (((1,), (1,)), ((), ()))
 TN = (((0,), (0,)), ((), ()))
@@ -64,7 +64,7 @@
     STF, STN, STY, TTF, TTN, TTY, TS,
     LG, L1s, L2s, INF, GP, GU, GC,
     BT, BRY, BRN, BRF, BS1, BG, BK, C1f, C2f,
-    GB, GRY, GZS, GRZ, GS2,
+    GB, GRY, GS1, GRN, GS2, GRF,
     ssem, rsem, lsem, tsem, isem, osem,
 ):
     d = lax.axis_index("dp")
@@ -115,7 +115,10 @@
     for k in FAR:
         pl.semaphore_signal(barrier, inc=1, device_id=y_dev(k), device_id_type=MESH)
         greeted += 1
-    for o in (8, 7, 9, 6, 10, 5, 11, 4, 12, 3, 13, 2, 14, 1, 15):
+    for k in FAR:
+        pl.semaphore_signal(barrier, inc=1, device_id=far_dev(k), device_id_type=MESH)
+        greeted += 1
+    for o in NEAR_FROM:
         pl.semaphore_signal(barrier, inc=1, device_id=near_dev(o), device_id_type=MESH)
         greeted += 1
     for k in range(1, 8):
@@ -449,25 +452,25 @@
 
     gh_y = []
 
-    def part(n):
-        for j in range(4 * n, 4 * n + 4):
-            zz = lax.rem(z + OFFS[j], 16)
-            product = dot(hwxT[pl.ds(pl.multiple_of(zz * 256, 256), 256), :], grad_ext)
+    def part(o):
+        at = lax.rem(zlo + o, 4)
+        for zh in range(4):
+            rows = pl.ds(pl.multiple_of((zh * 4 + at) * 256, 256), 256)
+            product = dot(hwxT[rows, :], grad_ext)
             for yy in range(4):
-                block = GB.at[yy, j]
+                block = GB.at[yy, at, zh]
                 piece = product[64 * yy : 64 * yy + 64]
                 block[0:64, :] = piece[:, 0:128].astype(BF16)
                 block[64:80, :] = pack_rest(piece[:, 128:256], 16).astype(BF16)
-        at = pl.ds(4 * n, 4)
         gh_y.append(
             [send(GB.at[lax.rem(y + k, 4), at], GRY.at[k - 1, at], y_dev(k)) for k in FAR]
         )
 
+    part(NEAR[0])
+    part(NEAR[2])
+    bk_f = small_far(BS1, BRN, bk_n, BRF)
+    part(NEAR[1])
     part(0)
-    part(1)
-    bk_f = small_far(BS1, BRN, bk_n, BRF)
-    part(2)
-    part(3)
     entries = jnp.where(rows_of((8, 256)) % 2 == 0, ge0, ge1).astype(BF16)
     full = dot(entries, WT[...], NT)
     pair = lax.div(rows_of((8, 1024)), 2)
@@ -477,26 +480,24 @@
     GC[d] = packed_cl
     GCv = GC.reshape(4, 2, 8, 1024)
     gc_x = dp_x(GCv)
+    order = (0, 2, 1)
+    gh_n = {}
+
+    def y_sum(at, ids):
+        for k, i in zip(FAR, ids):
+            recv(i, GRY.at[k - 1, at])
+        return (GB[y, at].astype(F32) + GRY[0, at].astype(F32)) + (
+            GRY[1, at].astype(F32) + GRY[2, at].astype(F32)
+        )
+
+    def chunk_near(turn_at):
+        n = order[turn_at]
+        GS1[n] = y_sum(lax.rem(zlo + NEAR[n], 4), gh_y[turn_at]).astype(BF16)
+        gh_n[n] = send(GS1.at[n], GRN.at[n], near_dev(NEAR[n]))
+
+    chunk_near(0)
     inf_c = dp_core(INFv, inf_x)
     gp_c = dp_core(GPv, gp_x)
-
-    gh_z = []
-
-    def chunk_z(n):
-        at = pl.ds(4 * n, 4)
-        for k, i in zip(FAR, gh_y[n]):
-            recv(i, GRY.at[k - 1, at])
-        for j in range(4 * n, 4 * n + 4):
-            total = (GB[y, j].astype(F32) + GRY[0, j].astype(F32)) + (
-                GRY[1, j].astype(F32) + GRY[2, j].astype(F32)
-            )
-            if OFFS[j]:
-                GZS[j] = total.astype(BF16)
-                gh_z.append(send(GZS.at[j], GRZ.at[j], near_dev(OFFS[j])))
-            else:
-                GS2[...] = total
-
-    chunk_z(0)
     def assemble(src, dst1, dst2):
         for g in range(8):
             both = src[g].astype(F32)
@@ -535,16 +536,29 @@
         gt2_ref[:, pl.ds(at, 128)] = dot(mine2, grads)
         return 0
 
-    chunk_z(1)
+    chunk_near(1)
     small_total(BRF, bk_f, BG)
     bk_bn = back_near_first(BG)
-    lax.fori_loop(0, 7, tail_two, 0)
-    chunk_z(2)
+    lax.fori_loop(0, 6, tail_two, 0)
+    chunk_near(2)
     bk_by = back_y_second(BG, bk_bn)
+    mine_sum = y_sum(zlo, gh_y[3])
+    for n in range(3):
+        recv(gh_n[n], GRN.at[n])
+    GS2[...] = mine_sum + (
+        GRN[0].astype(F32) + (GRN[1].astype(F32) + GRN[2].astype(F32))
+    )
+    for k in FAR:
+        GRF[2 + k] = GS2[lax.rem(zhi + k, 4)].astype(BF16)
+    gh_f = [send(GRF.at[2 + k], GRF.at[k - 1], far_dev(k)) for k in FAR]
+    small_done(BG, [(i, lax.rem(y + 4 - k, 4), None) for k, i in zip(FAR, bk_by)])
+    BK[d] = Xf[...].astype(BF16)
+    BKv = BK.reshape(4, 2, 80, 640)
+    bk_x = dp_x(BKv)
+
     gc_c = dp_core(GCv, gc_x)
-    lax.fori_loop(7, 13, tail_two, 0)
+    lax.fori_loop(6, 13, tail_two, 0)
     store(gt2_ref, gt2_out)
-    chunk_z(3)
     HG[d] = G[:, pl.ds(lax.rem(2 * d, 4), 2), lax.div(d, 2)]
     dp_done(GPv, gp_c)
     for k, i in zip(range(1, 8), slices):
@@ -569,11 +583,6 @@
     lax.fori_loop(0, 8, head_group, 0)
     store(head_ref, head_out)
 
-    small_done(BG, [(i, lax.rem(y + 4 - k, 4), None) for k, i in zip(FAR, bk_by)])
-    BK[d] = Xf[...].astype(BF16)
-    BKv = BK.reshape(4, 2, 80, 640)
-    bk_x = dp_x(BKv)
-
     dp_done(GCv, gc_c)
     cl_sum = ((GC[0] + GC[1]) + (GC[2] + GC[3])) + ((GC[4] + GC[5]) + (GC[6] + GC[7]))
     for k in range(4):
@@ -587,18 +596,17 @@
     hot2 = jnp.where(slot_hit[40:80], 1.0, 0.0)
     back_one = dot(p1_ref[:, 0:640], b1a, NT) + dot(p1_ref[:, 640:1024], b1b, NT)
     add = dot_exact(back_one, hot1) + dot_exact(dot(p2_ref[...], b2, NT), hot2)
-    block = GS2[...]
-    for j, i in enumerate(gh_z):
-        recv(i, GRZ.at[j])
-        block = block + GRZ[j].astype(F32)
+    bk_c = dp_core(BKv, bk_x)
+
+    for n, i in enumerate(gh_f):
+        recv(i, GRF.at[n])
+    block = GS2[zhi] + (GRF[0].astype(F32) + (GRF[1].astype(F32) + GRF[2].astype(F32)))
     hp[:, 0:128] = block[0:64, :]
     for q in range(4):
         part_q = block[64:80, :]
         hp[16 * q : 16 * q + 16, 128:256] = part_q if q == 0 else pltpu.roll(part_q, 128 - 32 * q, 1)
     gh_ref[...] = (hp[...] + add)[:, 0:160]
     store(gh_ref, gh_out)
-
-    bk_c = dp_core(BKv, bk_x)
 
     dp_done(CHv, ch_c)
     dp_done(BKv, bk_c)
@@ -652,8 +660,8 @@
         V((4, 4, 4, 8, 128), F32), V((3, 4, 4, 8, 128), F32), V((3, 4, 8, 128), F32), V((4, 4, 8, 128), F32),
         V((4, 4, 8, 128), F32), V((4, 4, 4, 8, 128), F32), V((8, 80, 640), BF16),
         V((320, 128), F32), V((320, 128), F32),
-        V((4, 16, 80, 128), BF16), V((3, 16, 80, 128), BF16), V((16, 80, 128), BF16),
-        V((16, 80, 128), BF16), V((80, 128), F32),
+        V((4, 4, 4, 80, 128), BF16), V((3, 4, 4, 80, 128), BF16), V((3, 4, 80, 128), BF16),
+        V((3, 4, 80, 128), BF16), V((4, 80, 128), F32), V((6, 80, 128), BF16),
         pltpu.SemaphoreType.DMA((SEMS,)), pltpu.SemaphoreType.DMA((SEMS,)), pltpu.SemaphoreType.DMA,
         pltpu.SemaphoreType.DMA((2,)), pltpu.SemaphoreType.DMA((7,)), pltpu.SemaphoreType.DMA((8,)),
     ]

time: 107 us -> 103 us (0.963)
  Pallas kernels: 106 us -> 102 us
    pallas_call x1, Pallas kernels: 104 us -> 99.7 us  [on_device(): pl.pallas_call(kernel, out_shape=[jax.ShapeDtypeStruct(s, t) for s, t in...]
where the time goes in v6:
time: 103 us
  Pallas kernels  102 us (99%)
    pallas_call x1, Pallas kernels, on_device(): pl.pallas_call(kernel, out_shape=[jax.ShapeDtypeStruct(s, t) for s, t in...  99.7 us
    pallas_call x1, Pallas kernels, on_device(): pl.pallas_call(hand_over, out_shape=[jax.ShapeDtypeStruct(s, t) for s, t...  2.27 us

profile of v6, /device:TPU:1, one launch (start us, length us, event | category | flops | bytes accessed | tf_op | source)
XLA Modules:
  0.0 102.6 jit_solution(9185320367227332252)
XLA Ops:
  0.6 99.7 %shard_map.170 = (f32[1,160]{1,0:T(1,128)}, f32[64,160]{1,0:T(8,128)}, f32[160,512]{1,0:T(8,128)}, f32[2,4096]{1,0:T(2,128)}, f32[64,1024]{1,0:T(8,128)}, /*inde...) custom-call(bf16[64,160]{1,0:T(8,128)(2,1)} %bitcast.7, bf16[160,4096]{1,0:T(8,128)(2,1)} %hw_ref.1, ...), custom_call_target="tpu_custom_call" | custom-call | tf_op jit(solution)/shard_map/pallas_call | solution.py:668
  100.3 2.3 %shard_map.171 = (f32[1,160]{1,0:T(1,128)}, f32[64,160]{1,0:T(8,128)}, f32[160,512]{1,0:T(8,128)}, f32[2,4096]{1,0:T(2,128)}, f32[64,1024]{1,0:T(8,128)}, /*inde...) custom-call(f32[1,160]{1,0:T(1,128)} %get-tuple-element.24.refs_0_, f32[64,160]{1,0:T(8,128)} %get-tuple-element.25.refs_1_, ...), custom_call_target="tpu_custom_call" | custom-call | tf_op jit(solution)/shard_map/pallas_call | solution.py:681

commit v7 on v6

--- a/solution.py
+++ b/solution.py
@@ -11,8 +11,8 @@
 SCALE = 64.0
 FAR = (1, 2, 3)
 NEAR = (1, 15, 2)
-NEAR_FROM = (15, 1, 14)
-SEMS = 144
+PAIRS = tuple((o, k) for o in (0,) + NEAR for k in (0,) + FAR)[1:]
+SEMS = 176
 NT = (((1,), (1,)), ((), ()))
 TN = (((0,), (0,)), ((), ()))
 NN = (((1,), (0,)), ((), ()))
@@ -61,7 +61,7 @@
     t1_ref, t2_ref, ids, hp, G, WT, hwx, hwxT, HG, HU,
     CH, PT, PRY, PRN, PRF, PS1, PG, Xf, PJ,
     P1f, P2f, P1b, P2b,
-    STF, STN, STY, TTF, TTN, TTY, TS,
+    STF, STN, TTF, TTN, TS,
     LG, L1s, L2s, INF, GP, GU, GC,
     BT, BRY, BRN, BRF, BS1, BG, BK, C1f, C2f,
     GB, GRY, GS1, GRN, GS2, GRF,
@@ -79,6 +79,9 @@
     def near_dev(o):
         return (d, lax.rem(z + o, 16) * 4 + y)
 
+    def pair_dev(o, k):
+        return (d, lax.rem(z + o, 16) * 4 + lax.rem(y + k, 4))
+
     def y_dev(k):
         return (d, z * 4 + lax.rem(y + k, 4))
 
@@ -113,13 +116,10 @@
     barrier = pltpu.get_barrier_semaphore()
     greeted = 0
     for k in FAR:
-        pl.semaphore_signal(barrier, inc=1, device_id=y_dev(k), device_id_type=MESH)
-        greeted += 1
-    for k in FAR:
         pl.semaphore_signal(barrier, inc=1, device_id=far_dev(k), device_id_type=MESH)
         greeted += 1
-    for o in NEAR_FROM:
-        pl.semaphore_signal(barrier, inc=1, device_id=near_dev(o), device_id_type=MESH)
+    for o, k in PAIRS:
+        pl.semaphore_signal(barrier, inc=1, device_id=pair_dev(16 - o, 4 - k), device_id_type=MESH)
         greeted += 1
     for k in range(1, 8):
         pl.semaphore_signal(barrier, inc=1, device_id=dp_dev(k), device_id_type=MESH)
@@ -224,25 +224,16 @@
             recv(i, fslots.at[lax.rem(zhi + 4 - k, 4)])
         full[y, zlo] = (fslots[0] + fslots[1]) + (fslots[2] + fslots[3])
 
-    def back_y_first(full):
-        return [send(full.at[y, zlo], full.at[y, zlo], y_dev(k)) for k in FAR]
-
-    def back_near_second(full, ids):
-        for k, i in zip(FAR, ids):
-            recv(i, full.at[lax.rem(y + 4 - k, 4), zlo])
-        return [send(full.at[:, zlo], full.at[:, zlo], near_dev(o)) for o in NEAR]
-
-    def back_near_first(full):
-        return [send(full.at[y, zlo], full.at[y, zlo], near_dev(o)) for o in NEAR]
-
-    def back_y_second(full, ids):
-        for o, i in zip(NEAR, ids):
-            recv(i, full.at[y, lax.rem(zlo + 16 - o, 4)])
-        return [send(full.at[y], full.at[y], y_dev(k)) for k in FAR]
-
-    def small_done(full, waits):
-        for i, yy, zl in waits:
-            recv(i, full.at[yy] if zl is None else full.at[yy, zl])
+    def pair_send(full):
+        own_entry = full.at[y, zlo]
+        return [send(own_entry, own_entry, pair_dev(o, k)) for o, k in PAIRS]
+
+    def pair_wait(full, ids):
+        for (o, k), i in zip(PAIRS, ids):
+            recv(i, full.at[lax.rem(y + 4 - k, 4), lax.rem(zlo + 16 - o, 4)])
+
+    def small_done(full, ids):
+        pair_wait(full, ids)
         for t in range(50):
             i, j = t // 10, t % 10
             r, l = (8 * i, 128 * j) if j < 5 else (40 + 8 * i, 128 * j - 640)
@@ -302,15 +293,14 @@
 
     pass_on(0)
     small_total(PRF, pr_f, PG)
-    pr_by = back_y_first(PG)
+    pr_all = pair_send(PG)
     pass_on(1)
     pass_on(2)
-    pr_bn = back_near_second(PG, pr_by)
     ch_c = dp_core(CHv, ch_x)
     lax.fori_loop(20, 32, turn, 0)
     for n in range(3):
         spread(y, lax.rem(zlo + 16 - NEAR[n], 4))
-    small_done(PG, [(i, slice(None), lax.rem(zlo + 16 - o, 4)) for o, i in zip(NEAR, pr_bn)])
+    small_done(PG, pr_all)
     PJ[d] = Xf[...].astype(BF16)
     PJv = PJ.reshape(4, 2, 80, 640)
     pj_x = dp_x(PJv)
@@ -340,13 +330,15 @@
     TTF[zhi] = jnp.transpose(TS[...])[0:8, :]
     tail_ids = [send(TTF.at[zhi], TTF.at[zhi], far_dev(k)) for k in FAR]
 
-    def join(slots):
-        parts = [slots[i] for i in range(4)]
-        m = [p[0:1] for p in parts]
-        top = jnp.maximum(jnp.maximum(m[0], m[1]), jnp.maximum(m[2], m[3]))
-        s = [p[1:2] * jnp.exp(mm - top) for p, mm in zip(parts, m)]
-        t = [p[2:3] for p in parts]
-        return top, (s[0] + s[1]) + (s[2] + s[3]), (t[0] + t[1]) + (t[2] + t[3])
+    def join(parts):
+        top = parts[0][0:1]
+        for p in parts[1:]:
+            top = jnp.maximum(top, p[0:1])
+        total, picked = 0.0, 0.0
+        for p in parts:
+            total = total + p[1:2] * jnp.exp(p[0:1] - top)
+            picked = picked + p[2:3]
+        return top, total, picked
 
     def as_tile(result):
         row = rows_of((8, result[0].shape[1]))
@@ -357,19 +349,12 @@
     def join_far(far, near, ids):
         for k, i in zip(FAR, ids):
             recv(i, far.at[lax.rem(zhi + 4 - k, 4)])
-        near[zlo] = as_tile(join(far))
-        return [send(near.at[zlo], near.at[zlo], near_dev(o)) for o in NEAR]
-
-    def join_near(near, last, ids):
-        for o, i in zip(NEAR, ids):
-            recv(i, near.at[lax.rem(zlo + 16 - o, 4)])
-        last[y] = as_tile(join(near))
-        return [send(last.at[y], last.at[y], y_dev(k)) for k in FAR]
-
-    def join_last(last, ids):
-        for k, i in zip(FAR, ids):
-            recv(i, last.at[lax.rem(y + 4 - k, 4)])
-        return join(last)
+        near[y, zlo] = as_tile(join([far[n] for n in range(4)]))
+        return pair_send(near)
+
+    def join_all(near, ids):
+        pair_wait(near, ids)
+        return join([near[m, n] for m in range(4) for n in range(4)])
 
 
     for n, ids_y in enumerate(hid_y):
@@ -396,9 +381,7 @@
     head_ids = [send(STF.at[zhi], STF.at[zhi], far_dev(k)) for k in FAR]
     tail_ids = join_far(TTF, TTN, tail_ids)
     pj_c = dp_core(PJv, pj_x)
-    tail_ids = join_near(TTN, TTY, tail_ids)
-    head_ids = join_far(STF, STN, head_ids)
-    tail_stats = join_last(TTY, tail_ids)
+    tail_stats = join_all(TTN, tail_ids)
 
     tail_lse = tail_stats[0] + jnp.log(tail_stats[1])
     TS[...] = jnp.zeros_like(TS)
@@ -417,12 +400,12 @@
     to_tiles(BT, dot(own1, t1_ref[...]), dot(own2, t2_ref[...]))
     bk_y = small_y(BT, BRY)
 
-    head_ids = join_near(STN, STY, head_ids)
+    head_ids = join_far(STF, STN, head_ids)
     INF[d] = jnp.where(lane == 0, lse_col, jnp.where(lane == 1, goal.astype(F32), 0.0))
     INFv = INF.reshape(4, 2, 80, 128)
     inf_x = dp_x(INFv)
     bk_n = small_near(BT, BRY, bk_y, BS1, BRN)
-    stats = join_last(STY, head_ids)
+    stats = join_all(STN, head_ids)
 
     entry0, entry1 = LG[160:161, :], LG[161:162, :]
     top = jnp.maximum(stats[0], jnp.maximum(entry0, entry1))
@@ -538,10 +521,9 @@
 
     chunk_near(1)
     small_total(BRF, bk_f, BG)
-    bk_bn = back_near_first(BG)
+    bk_all = pair_send(BG)
     lax.fori_loop(0, 6, tail_two, 0)
     chunk_near(2)
-    bk_by = back_y_second(BG, bk_bn)
     mine_sum = y_sum(zlo, gh_y[3])
     for n in range(3):
         recv(gh_n[n], GRN.at[n])
@@ -551,7 +533,7 @@
     for k in FAR:
         GRF[2 + k] = GS2[lax.rem(zhi + k, 4)].astype(BF16)
     gh_f = [send(GRF.at[2 + k], GRF.at[k - 1], far_dev(k)) for k in FAR]
-    small_done(BG, [(i, lax.rem(y + 4 - k, 4), None) for k, i in zip(FAR, bk_by)])
+    small_done(BG, bk_all)
     BK[d] = Xf[...].astype(BF16)
     BKv = BK.reshape(4, 2, 80, 640)
     bk_x = dp_x(BKv)
@@ -653,8 +635,8 @@
         V((3, 4, 8, 128), F32), V((4, 4, 8, 128), F32), V((4, 4, 8, 128), F32),
         V((4, 4, 4, 8, 128), F32), V((80, 640), F32), V((8, 80, 640), BF16),
         V((320, 1024), F32), V((320, 256), F32), V((320, 1024), BF16), V((320, 256), BF16),
-        V((4, 8, 256), F32), V((4, 8, 256), F32), V((4, 8, 256), F32),
-        V((4, 8, 128), F32), V((4, 8, 128), F32), V((4, 8, 128), F32), V((128, 128), F32),
+        V((4, 8, 256), F32), V((4, 4, 8, 256), F32),
+        V((4, 8, 128), F32), V((4, 4, 8, 128), F32), V((128, 128), F32),
         V((256, 256), F32), V((40, 320), F32), V((40, 1664), F32), V((8, 80, 128), F32),
         V((8, 208, 128), BF16), V((160, 256), BF16), V((8, 8, 1024), F32),
         V((4, 4, 4, 8, 128), F32), V((3, 4, 4, 8, 128), F32), V((3, 4, 8, 128), F32), V((4, 4, 8, 128), F32),

time: 103 us -> 100 us (0.971)
  Pallas kernels: 102 us -> 99.5 us
    pallas_call x1, Pallas kernels: 99.7 us -> 97.2 us  [on_device(): pl.pallas_call(kernel, out_shape=[jax.ShapeDtypeStruct(s, t) for s, t in...]
where the time goes in v7:
time: 100 us
  Pallas kernels  99.5 us (100%)
    pallas_call x1, Pallas kernels, on_device(): pl.pallas_call(kernel, out_shape=[jax.ShapeDtypeStruct(s, t) for s, t in...  97.2 us
    pallas_call x1, Pallas kernels, on_device(): pl.pallas_call(hand_over, out_shape=[jax.ShapeDtypeStruct(s, t) for s, t...  2.27 us

profile of v7, /device:TPU:1, one launch (start us, length us, event | category | flops | bytes accessed | tf_op | source)
XLA Modules:
  0.0 100.1 jit_solution(12550477500891782499)
XLA Ops:
  0.6 97.2 %shard_map.170 = (f32[1,160]{1,0:T(1,128)}, f32[64,160]{1,0:T(8,128)}, f32[160,512]{1,0:T(8,128)}, f32[2,4096]{1,0:T(2,128)}, f32[64,1024]{1,0:T(8,128)}, /*inde...) custom-call(bf16[64,160]{1,0:T(8,128)(2,1)} %bitcast.7, bf16[160,4096]{1,0:T(8,128)(2,1)} %hw_ref.1, ...), custom_call_target="tpu_custom_call" | custom-call | tf_op jit(solution)/shard_map/pallas_call | solution.py:650
  97.9 2.3 %shard_map.171 = (f32[1,160]{1,0:T(1,128)}, f32[64,160]{1,0:T(8,128)}, f32[160,512]{1,0:T(8,128)}, f32[2,4096]{1,0:T(2,128)}, f32[64,1024]{1,0:T(8,128)}, /*inde...) custom-call(f32[1,160]{1,0:T(1,128)} %get-tuple-element.24.refs_0_, f32[64,160]{1,0:T(8,128)} %get-tuple-element.25.refs_1_, ...), custom_call_target="tpu_custom_call" | custom-call | tf_op jit(solution)/shard_map/pallas_call | solution.py:663

commit v8 on v7

--- a/solution.py
+++ b/solution.py
@@ -291,9 +291,9 @@
         recv(hid_near[n], G.at[y, at])
         hid_y.append([send(G.at[y, at], G.at[y, at], y_dev(k)) for k in FAR])
 
-    pass_on(0)
     small_total(PRF, pr_f, PG)
     pr_all = pair_send(PG)
+    pass_on(0)
     pass_on(1)
     pass_on(2)
     ch_c = dp_core(CHv, ch_x)

time: 100 us -> 99 us (0.990)
  Pallas kernels: 99.5 us -> 98.1 us
    pallas_call x1, Pallas kernels: 97.2 us -> 95.9 us  [on_device(): pl.pallas_call(kernel, out_shape=[jax.ShapeDtypeStruct(s, t) for s, t in...]
where the time goes in v8:
time: 99 us; the launch traced here: 98.8 us
  Pallas kernels  98.1 us (99%)
    pallas_call x1, Pallas kernels, on_device(): pl.pallas_call(kernel, out_shape=[jax.ShapeDtypeStruct(s, t) for s, t in...  95.9 us
    pallas_call x1, Pallas kernels, on_device(): pl.pallas_call(hand_over, out_shape=[jax.ShapeDtypeStruct(s, t) for s, t...  2.27 us

profile of v8, /device:TPU:1, one launch (start us, length us, event | category | flops | bytes accessed | tf_op | source)
XLA Modules:
  0.0 98.8 jit_solution(4100560953928602993)
XLA Ops:
  0.6 95.9 %shard_map.170 = (f32[1,160]{1,0:T(1,128)}, f32[64,160]{1,0:T(8,128)}, f32[160,512]{1,0:T(8,128)}, f32[2,4096]{1,0:T(2,128)}, f32[64,1024]{1,0:T(8,128)}, /*inde...) custom-call(bf16[64,160]{1,0:T(8,128)(2,1)} %bitcast.7, bf16[160,4096]{1,0:T(8,128)(2,1)} %hw_ref.1, ...), custom_call_target="tpu_custom_call" | custom-call | tf_op jit(solution)/shard_map/pallas_call | solution.py:650
  96.5 2.3 %shard_map.171 = (f32[1,160]{1,0:T(1,128)}, f32[64,160]{1,0:T(8,128)}, f32[160,512]{1,0:T(8,128)}, f32[2,4096]{1,0:T(2,128)}, f32[64,1024]{1,0:T(8,128)}, /*inde...) custom-call(f32[1,160]{1,0:T(1,128)} %get-tuple-element.24.refs_0_, f32[64,160]{1,0:T(8,128)} %get-tuple-element.25.refs_1_, ...), custom_call_target="tpu_custom_call" | custom-call | tf_op jit(solution)/shard_map/pallas_call | solution.py:663
